TPU v7x, 32 devices: a whole 2x2x4 slice. The times are simulated.
32 devices in a mesh: seq: 16 (over z, x, core), tp: 2 (over y).
Axes of the slice: x: 2, y: 2, z: 4, core: 2. Of those that a mesh axis runs over, the one named last changes fastest.
Arguments:
- layer_input: bfloat16 [4608, 896], P('seq'), may hold values from -6 to 6
- block_order: int32 [32], replicated, may hold values from 0 to 31, each once
- attn_gain: float32 [896], replicated, may hold values from 0.5 to 1.5
- query_weight: bfloat16 [896, 896], P(None, 'tp'), may hold values from -0.1875 to 0.1875
- query_bias: float32 [896], P('tp'), may hold values from -3 to 3
- key_weight: bfloat16 [896, 128], P(None, 'tp'), may hold values from -0.1875 to 0.1875
- key_bias: float32 [128], P('tp'), may hold values from -3 to 3
- value_weight: bfloat16 [896, 128], P(None, 'tp'), may hold values from -0.1875 to 0.1875
- value_bias: float32 [128], P('tp'), may hold values from -1.2 to 1.2
- out_weight: bfloat16 [896, 896], P('tp'), may hold values from -1.5 to 1.5
- mlp_gain: float32 [896], replicated, may hold values from 0.5 to 1.5
- gate_weight: bfloat16 [896, 4864], P(None, 'tp'), may hold values from -0.1875 to 0.1875
- up_weight: bfloat16 [896, 4864], P(None, 'tp'), may hold values from -0.1875 to 0.1875
- down_weight: bfloat16 [4864, 896], P('tp'), may hold values from -0.078125 to 0.078125
- out_cotangent: bfloat16 [4608, 896], P('seq'), may hold values from -6 to 6
Outputs:
- layer_output: bfloat16 [4608, 896], P('seq')
- input_grad: bfloat16 [4608, 896], P('seq')
- attn_gain_grad: float32 [896], replicated
- query_weight_grad: float32 [896, 896], P(None, 'tp')
- query_bias_grad: float32 [896], P('tp')
- key_weight_grad: float32 [896, 128], P(None, 'tp')
- key_bias_grad: float32 [128], P('tp')
- value_weight_grad: float32 [896, 128], P(None, 'tp')
- value_bias_grad: float32 [128], P('tp')
- out_weight_grad: float32 [896, 896], P('tp')
- mlp_gain_grad: float32 [896], replicated
- gate_weight_grad: float32 [896, 4864], P(None, 'tp')
- up_weight_grad: float32 [896, 4864], P(None, 'tp')
- down_weight_grad: float32 [4864, 896], P('tp')
Inputs may be any that keep to these rules, and one draw needn't show every extreme that they name: `block_order`: A permutation: each of the 32 blocks of 144 consecutive positions stands in exactly one slot.
All inputs are finite; a program needn't handle non-finite values.
Results may differ from a plain program's by a relative error of at most 0.03.
Values may be sent and summed in bfloat16 or wider, within the bound.
A program may use at most 192 MiB of HBM per device.

v0:
```python
import jax
import jax.numpy as jnp
from jax import lax
from jax.sharding import PartitionSpec as P

HEAD_DIM = 64


EPSILON = 1e-06
NEGATIVE = -1e30
ROPE_BASE = 1000000.0


def pick_block(total, largest):
    chosen = 1
    for candidate in range(1, min(total, largest) + 1):
        if total % candidate == 0:
            chosen = candidate
    return chosen


def rope_tables(positions, head_size):
    half_size = head_size // 2
    exponent = jnp.arange(half_size, dtype=jnp.float32) * (2.0 / head_size)
    frequency = jnp.power(ROPE_BASE, -exponent)
    angle = positions.astype(jnp.float32)[:, None] * frequency[None, :]
    return (jnp.cos(angle)[:, None, :], jnp.sin(angle)[:, None, :])


def rotate(values, cosine, sine):
    half_size = values.shape[-1] // 2
    first = values[..., :half_size]
    second = values[..., half_size:]
    return jnp.concatenate(
        [first * cosine - second * sine, second * cosine + first * sine], axis=-1
    )


def rms_forward(values):
    factor = lax.rsqrt(jnp.mean(values * values, axis=-1, keepdims=True) + EPSILON)
    return (values * factor, factor)


def rms_backward(grad_normed, normed, factor, gain):
    gain_grad = jnp.sum(grad_normed * normed, axis=0)
    weighted = grad_normed * gain
    values_grad = factor * (weighted - normed * jnp.mean(weighted * normed, axis=-1, keepdims=True))
    return (gain_grad, values_grad)


def key_sweep(visit_block, initial, kv_all, key_places, block_rows):
    block_count = kv_all.shape[0] // block_rows

    def visit(carry, number):
        kv_block = lax.dynamic_slice_in_dim(kv_all, number * block_rows, block_rows, 0)
        places = lax.dynamic_slice_in_dim(key_places, number * block_rows, block_rows, 0)
        return visit_block(carry, kv_block, places)

    return lax.scan(visit, initial, jnp.arange(block_count, dtype=jnp.int32))


def per_device(
    layer_input,
    block_order,
    attn_gain,
    query_weight,
    query_bias,
    key_weight,
    key_bias,
    value_weight,
    value_bias,
    out_weight,
    mlp_gain,
    gate_weight,
    up_weight,
    down_weight,
    out_cotangent,
):
    row_count = layer_input.shape[0]
    head_size = HEAD_DIM
    key_heads = key_weight.shape[1] // head_size
    key_width = key_heads * head_size
    group_size = query_weight.shape[1] // key_width
    block_rows = row_count // 2
    score_scale = head_size ** (-0.5)
    seq_index = lax.axis_index("seq")
    own_slots = lax.dynamic_slice_in_dim(block_order, 2 * seq_index, 2)
    steps_in = jnp.arange(block_rows, dtype=jnp.int32)
    own_places = (own_slots[:, None] * block_rows + steps_in[None, :]).reshape(-1)
    key_places = (block_order[:, None] * block_rows + steps_in[None, :]).reshape(-1)
    cosine, sine = rope_tables(own_places, head_size)
    inputs = layer_input.astype(jnp.float32)
    normed_first, factor_first = rms_forward(inputs)
    normed_attn = (normed_first * attn_gain).astype(jnp.bfloat16)
    query_rows = (
        jnp.dot(normed_attn, query_weight, preferred_element_type=jnp.float32) + query_bias
    ).reshape(row_count, key_heads * group_size, head_size)
    key_rows = (
        jnp.dot(normed_attn, key_weight, preferred_element_type=jnp.float32) + key_bias
    ).reshape(row_count, key_heads, head_size)
    value_rows = (
        jnp.dot(normed_attn, value_weight, preferred_element_type=jnp.float32) + value_bias
    ).astype(jnp.bfloat16)
    query_rot = (
        rotate(query_rows, cosine, sine)
        .astype(jnp.bfloat16)
        .reshape(row_count, key_heads, group_size, head_size)
    )
    key_rot = rotate(key_rows, cosine, sine).astype(jnp.bfloat16).reshape(row_count, key_width)
    kv_own = jnp.concatenate([key_rot, value_rows], axis=1)
    kv_all = lax.all_gather(kv_own, "seq", axis=0, tiled=True)
    key_block_rows = pick_block(kv_all.shape[0], 2048)

    def key_scores(kv_block, places):
        key_block = kv_block[:, :key_width].reshape(-1, key_heads, head_size)
        value_block = kv_block[:, key_width:].reshape(-1, key_heads, head_size)
        scores = (
            jnp.einsum("qcgd,kcd->cgqk", query_rot, key_block, preferred_element_type=jnp.float32)
            * score_scale
        )
        visible = places[None, :] <= own_places[:, None]
        return (scores, visible, key_block, value_block)

    def stats_block(carry, kv_block, places):
        running_max, running_sum = carry
        scores, visible, key_block, value_block = key_scores(kv_block, places)
        scores = jnp.where(visible, scores, NEGATIVE)
        new_max = jnp.maximum(running_max, jnp.max(scores, axis=-1))
        shifted = jnp.exp(jnp.where(visible, scores - new_max[..., None], NEGATIVE))
        running_sum = running_sum * jnp.exp(running_max - new_max) + jnp.sum(shifted, axis=-1)
        return ((new_max, running_sum), None)

    stat_shape = (key_heads, group_size, row_count)
    stats_start = (jnp.full(stat_shape, NEGATIVE, jnp.float32), jnp.zeros(stat_shape, jnp.float32))
    (running_max, running_sum), unused = key_sweep(
        stats_block, stats_start, kv_all, key_places, key_block_rows
    )
    log_total = running_max + jnp.log(running_sum)

    def output_block(carry, kv_block, places):
        scores, visible, key_block, value_block = key_scores(kv_block, places)
        weights_low = jnp.exp(jnp.where(visible, scores - log_total[..., None], NEGATIVE)).astype(
            jnp.bfloat16
        )
        return (
            carry
            + jnp.einsum(
                "cgqk,kcd->qcgd", weights_low, value_block, preferred_element_type=jnp.float32
            ),
            None,
        )

    attention_start = jnp.zeros((row_count, key_heads, group_size, head_size), jnp.float32)
    attention, unused = key_sweep(output_block, attention_start, kv_all, key_places, key_block_rows)
    attention_low = attention.reshape(row_count, -1).astype(jnp.bfloat16)
    attn_branch = lax.psum(
        jnp.dot(attention_low, out_weight, preferred_element_type=jnp.float32).astype(jnp.bfloat16),
        "tp",
    ).astype(jnp.float32)
    resid = inputs + attn_branch
    normed_second, factor_second = rms_forward(resid)
    normed_mlp = (normed_second * mlp_gain).astype(jnp.bfloat16)
    gate = jnp.dot(normed_mlp, gate_weight, preferred_element_type=jnp.float32)
    upward = jnp.dot(normed_mlp, up_weight, preferred_element_type=jnp.float32)
    silu_gate = jax.nn.silu(gate)
    mixed = (silu_gate * upward).astype(jnp.bfloat16)
    mlp_branch = lax.psum(
        jnp.dot(mixed, down_weight, preferred_element_type=jnp.float32).astype(jnp.bfloat16), "tp"
    ).astype(jnp.float32)
    layer_output = (resid + mlp_branch).astype(jnp.bfloat16)
    grad_output = out_cotangent.astype(jnp.float32)
    down_grad = jnp.einsum("rf,rd->fd", mixed, out_cotangent, preferred_element_type=jnp.float32)
    grad_mixed = jnp.einsum(
        "rd,fd->rf", out_cotangent, down_weight, preferred_element_type=jnp.float32
    )
    sigmoid_gate = jax.nn.sigmoid(gate)
    grad_gate = (grad_mixed * upward * sigmoid_gate * (1.0 + gate * (1.0 - sigmoid_gate))).astype(
        jnp.bfloat16
    )
    grad_upward = (grad_mixed * silu_gate).astype(jnp.bfloat16)
    gate_grad = jnp.einsum("rd,rf->df", normed_mlp, grad_gate, preferred_element_type=jnp.float32)
    up_grad = jnp.einsum("rd,rf->df", normed_mlp, grad_upward, preferred_element_type=jnp.float32)
    grad_normed_mlp = jnp.einsum(
        "rf,df->rd", grad_gate, gate_weight, preferred_element_type=jnp.float32
    ) + jnp.einsum("rf,df->rd", grad_upward, up_weight, preferred_element_type=jnp.float32)
    grad_normed_mlp = lax.psum(grad_normed_mlp.astype(jnp.bfloat16), "tp").astype(jnp.float32)
    mlp_gain_grad, grad_resid_part = rms_backward(
        grad_normed_mlp, normed_second, factor_second, mlp_gain
    )
    grad_resid = grad_output + grad_resid_part
    grad_branch = grad_resid.astype(jnp.bfloat16)
    out_grad = jnp.einsum(
        "rh,rd->hd", attention_low, grad_branch, preferred_element_type=jnp.float32
    )
    grad_attention = (
        jnp.einsum("rd,hd->rh", grad_branch, out_weight, preferred_element_type=jnp.float32)
        .astype(jnp.bfloat16)
        .reshape(row_count, key_heads, group_size, head_size)
    )
    delta = jnp.einsum("qcgd,qcgd->cgq", grad_attention.astype(jnp.float32), attention)

    def back_block(carry, kv_block, places):
        scores, visible, key_block, value_block = key_scores(kv_block, places)
        weights_full = jnp.exp(jnp.where(visible, scores - log_total[..., None], NEGATIVE))
        weights_low = weights_full.astype(jnp.bfloat16)
        grad_weights = jnp.einsum(
            "qcgd,kcd->cgqk", grad_attention, value_block, preferred_element_type=jnp.float32
        )
        grad_scores = (weights_full * (grad_weights - delta[..., None])).astype(jnp.bfloat16)
        carry = carry + jnp.einsum(
            "cgqk,kcd->qcgd", grad_scores, key_block, preferred_element_type=jnp.float32
        )
        grad_keys = (
            jnp.einsum("cgqk,qcgd->kcd", grad_scores, query_rot, preferred_element_type=jnp.float32)
            * score_scale
        )
        grad_values = jnp.einsum(
            "cgqk,qcgd->kcd", weights_low, grad_attention, preferred_element_type=jnp.float32
        )
        block_count = kv_block.shape[0]
        return (
            carry,
            jnp.concatenate(
                [
                    grad_keys.reshape(block_count, key_width),
                    grad_values.reshape(block_count, key_width),
                ],
                axis=1,
            ),
        )

    grad_query_sum, grad_kv_blocks = key_sweep(
        back_block, attention_start, kv_all, key_places, key_block_rows
    )
    grad_kv_terms = grad_kv_blocks.reshape(kv_all.shape[0], kv_all.shape[1])
    grad_kv_own = lax.psum_scatter(grad_kv_terms, "seq", scatter_dimension=0, tiled=True)
    grad_query_rot = (grad_query_sum * score_scale).reshape(
        row_count, key_heads * group_size, head_size
    )
    grad_query = rotate(grad_query_rot, cosine, -sine).reshape(row_count, -1).astype(jnp.bfloat16)
    grad_key = (
        rotate(grad_kv_own[:, :key_width].reshape(row_count, key_heads, head_size), cosine, -sine)
        .reshape(row_count, key_width)
        .astype(jnp.bfloat16)
    )
    grad_value = grad_kv_own[:, key_width:].astype(jnp.bfloat16)
    query_grad = jnp.einsum(
        "rd,rh->dh", normed_attn, grad_query, preferred_element_type=jnp.float32
    )
    key_grad = jnp.einsum("rd,rh->dh", normed_attn, grad_key, preferred_element_type=jnp.float32)
    value_grad = jnp.einsum(
        "rd,rh->dh", normed_attn, grad_value, preferred_element_type=jnp.float32
    )
    query_bias_grad = jnp.sum(grad_query.astype(jnp.float32), axis=0)
    key_bias_grad = jnp.sum(grad_key.astype(jnp.float32), axis=0)
    value_bias_grad = jnp.sum(grad_value.astype(jnp.float32), axis=0)
    grad_normed_attn = (
        jnp.einsum("rh,dh->rd", grad_query, query_weight, preferred_element_type=jnp.float32)
        + jnp.einsum("rh,dh->rd", grad_key, key_weight, preferred_element_type=jnp.float32)
        + jnp.einsum("rh,dh->rd", grad_value, value_weight, preferred_element_type=jnp.float32)
    )
    grad_normed_attn = lax.psum(grad_normed_attn.astype(jnp.bfloat16), "tp").astype(jnp.float32)
    attn_gain_grad, grad_input_part = rms_backward(
        grad_normed_attn, normed_first, factor_first, attn_gain
    )
    input_grad = (grad_resid + grad_input_part).astype(jnp.bfloat16)
    every_sum = lax.psum(
        (
            attn_gain_grad,
            query_grad,
            query_bias_grad,
            key_grad,
            key_bias_grad,
            value_grad,
            value_bias_grad,
            out_grad,
            gate_grad,
            up_grad,
            down_grad,
            mlp_gain_grad,
        ),
        "seq",
    )
    summed_attn = every_sum[:8]
    summed_mlp = every_sum[8:]
    return (
        layer_output,
        input_grad,
        summed_attn[0],
        summed_attn[1],
        summed_attn[2],
        summed_attn[3],
        summed_attn[4],
        summed_attn[5],
        summed_attn[6],
        summed_attn[7],
        summed_mlp[3],
        summed_mlp[0],
        summed_mlp[1],
        summed_mlp[2],
    )


def solution(mesh):
    placed = (
        P("seq", None),
        P(),
        P(),
        P(None, "tp"),
        P("tp"),
        P(None, "tp"),
        P("tp"),
        P(None, "tp"),
        P("tp"),
        P("tp", None),
        P(),
        P(None, "tp"),
        P(None, "tp"),
        P("tp", None),
        P("seq", None),
    )
    return jax.shard_map(
        per_device,
        mesh=mesh,
        in_specs=placed,
        out_specs=(
            P("seq", None),
            P("seq", None),
            P(),
            P(None, "tp"),
            P("tp"),
            P(None, "tp"),
            P("tp"),
            P(None, "tp"),
            P("tp"),
            P("tp", None),
            P(),
            P(None, "tp"),
            P(None, "tp"),
            P("tp", None),
        ),
        check_vma=False,
    )
```

profile of v0, /device:TPU:0, one launch (start us, length us, event | category | flops | bytes accessed | tf_op | source)
XLA Modules:
  0.0 920.3 jit_solution(12507099516063725013)
XLA Ops:
  17.5 37.1 %all-gather.2.cloned.1.call-done = bf16[4608,128]{1,0:T(8,128)(2,1)} async-done(((bf16[288,128]{1,0:T(8,128)(2,1)}), bf16[4608,128]{1,0:T(8,128)(2,1)}) %all-gather.2.cloned.1.call-update) | async-done | bytes 1179664 | tf_op jit(solution)/shard_map/all_gather | solution.py:111
  57.0 27.6 %while.37 = (s32[]{:T(128)}, f32[1,7,288]{2,1,0:T(8,128)S(1)}, f32[1,7,288]{2,1,0:T(8,128)S(1)}, s32[3]{0:T(128)S(1)}, s32[4608]{0:T(1024)S(1)}, /*index=5*/bf16...) while((s32[]{:T(128)}, f32[1,7,288]{2,1,0:T(8,128)S(1)}, ...), condition=%wide.region_4.5_spmd.clone, body=%wide.region_1.4_spmd.clone.sunk | while | flops 421587072 | bytes 26682448 | solution.py:59
  85.2 23.1 %while.38 = (s32[]{:T(128)}, f32[288,1,7,64]{0,3,2,1:T(8,128)S(1)}, s32[3]{0:T(128)S(1)}, bf16[4608,128]{0,1:T(8,128)(2,1)}, s32[4608]{0:T(1024)S(1)}, /*index=5...) while((s32[]{:T(128)}, f32[288,1,7,64]{0,3,2,1:T(8,128)S(1)}, ...), condition=%wide.region_6.7_spmd.clone, body=%wide.region_5.6_spmd.clone.sunk | while | flops 805810496 | bytes 2605792 | solution.py:59
  87.0 5.9 fusion.187
  94.7 5.9 fusion.187
  102.4 5.9 fusion.187
  110.0 27.3 %all-reduce.8.cloned.1.call-done = bf16[288,896]{1,0:T(8,128)(2,1)} async-done(((bf16[288,896]{1,0:T(8,128)(2,1)}), bf16[288,896]{1,0:T(8,128)(2,1)}) %all-reduce.8.cloned.1.call-update) | async-done | bytes 516112 | tf_op jit(solution)/shard_map/psum | solution.py:156
  154.5 28.7 %all-reduce.10.cloned.1.call-done = bf16[288,896]{1,0:T(8,128)(2,1)} async-done(((bf16[288,896]{1,0:T(8,128)(2,1)}), bf16[288,896]{1,0:T(8,128)(2,1)}) %all-reduce.10.cloned.1.call-update) | async-done | bytes 516112 | tf_op jit(solution)/shard_map/psum | solution.py:186
  189.3 62.4 %while.39 = (s32[]{:T(128)}, f32[288,1,7,64]{0,3,2,1:T(8,128)}, f32[3,1536,128]{2,1,0:T(8,128)}, s32[3]{0:T(128)S(1)}, bf16[4608,128]{0,1:T(8,128)(2,1)}, /*inde...) while((s32[]{:T(128)}, f32[288,1,7,64]{0,3,2,1:T(8,128)}, ...), condition=%wide.region_13.14_spmd.clone, body=%wide.region_12.13_spmd.clone.sunk | while | flops 2013769984 | bytes 71064152 | solution.py:59
  194.3 5.1 fusion.198
  199.4 5.3 fusion.196
  214.9 5.1 fusion.198
  220.0 5.3 fusion.196
  235.6 5.1 fusion.198
  240.7 5.3 fusion.196
  252.0 5.2 convolution_convert_fusion
  257.2 6.0 fusion.134
  263.3 6.0 fusion.133
  269.4 6.1 fusion.135
  276.9 38.1 %reduce-scatter.4.cloned.1.call-done = f32[288,128]{1,0:T(8,128)} async-done(((f32[4608,128]{1,0:T(8,128)}), f32[288,128]{1,0:T(8,128)}) %reduce-scatter.4.cloned.1.call-update) | async-done | bytes 147472
  332.1 30.6 %all-reduce.14.cloned.1.call-done = (bf16[288,896]{1,0:T(8,128)(2,1)}, bf16[288,896]{1,0:T(8,128)(2,1)}) async-done(((bf16[288,896]{1,0:T(8,128)(2,1)}, bf16[288,896]{1,0:T(8,128)(2,1)}), (bf16[288,896]{1,0:T(8,128)(2,1)}, bf16[288,896]{1,0:T(8,128)(2,1)})) %all-reduce.14.cloned.1.call-update) | async-done | bytes 1032208 | tf_op jit(solution)/shard_map/psum | solution.py:167
  364.3 64.3 %all-reduce = (f32[896]{0:T(1024)}, f32[448]{0:T(512)}, f32[64]{0:T(128)}, f32[64]{0:T(128)}, f32[896]{0:T(1024)}) all-reduce(f32[896]{0:T(1024)S(1)} %get-tuple-element.301, f32[448]{0:T(512)S(1)} %reduce_sum.100, f32[64]{0:T(128)S(1)} %get-tuple-element.392, ...), channel_id=1, replica_groups=mesh['seq'=16,'tp'=2] {'seq'}, use_global_device_ids=true, to_apply=%region_18.19 | all-reduce | flops 2368 | bytes 18944 | tf_op jit(solution)/shard_map/psum | solution.py:267
  431.6 456.1 %all-reduce.12.cloned.1.call-done = (f32[896,448]{0,1:T(8,128)}, f32[896,64]{0,1:T(8,128)}, f32[896,64]{0,1:T(8,128)}, f32[448,896]{1,0:T(8,128)}, f32[896,2432]...) async-done(((f32[896,448]{0,1:T(8,128)}, f32[896,64]{0,1:T(8,128)}, f32[896,64]{0,1:T(8,128)}, f32[448,896]{1,0:T(8,128)}, f32[896,2432]{1,0:T(8,128)}, ...) | async-done | bytes 29818896 | tf_op jit(solution)/shard_map/psum | solution.py:267
  895.0 8.6 copy.113
  (273 shorter events, 135.3 us)
Async XLA Ops:
  7.2 101.3 %copy-start = (bf16[448,896]{1,0:T(8,128)(2,1)S(1)}, bf16[448,896]{1,0:T(8,128)(2,1)}, u32[]{:S(2)}) copy-start(bf16[448,896]{1,0:T(8,128)(2,1)} %param.30) | copy-start | bytes 2408452
  7.2 47.4 %all-gather.2.cloned.1.call-start = ((), (), s32[]{:S(2)}) async-start(), calls=%async_computation.1 | async-start | bytes 1253376 | tf_op jit(solution)/shard_map/all_gather | solution.py:111
  7.3 10.1 %copy-start.39 = (f32[32]{0:T(128)}, f32[32]{0:T(128)S(1)}, u32[]{:S(2)}) copy-start(f32[32]{0:T(128)S(1)} %negate_power_fusion) | copy-start | bytes 388
  8.2 9.3 %copy-start.31 = (f32[288]{0:T(512)}, f32[288]{0:T(512)S(1)}, u32[]{:S(2)}) copy-start(f32[288]{0:T(512)S(1)} %convert_element_type.123) | copy-start | bytes 3460
  13.5 123.8 %all-reduce.8.cloned.1.call-start = ((), (), s32[]{:S(2)}) async-start(), calls=%async_computation.2 | async-start | bytes 1032192 | tf_op jit(solution)/shard_map/psum | solution.py:156
  17.3 39.7 %copy-start.26 = (f32[288,32]{0,1:T(8,128)}, f32[288,32]{0,1:T(8,128)S(1)}, u32[]{:S(2)}) copy-start(f32[288,32]{0,1:T(8,128)S(1)} %get-tuple-element.390) | copy-start | bytes 110596
  85.2 52.1 %copy-start.2 = (bf16[288,896]{1,0:T(8,128)(2,1)S(1)}, bf16[288,896]{1,0:T(8,128)(2,1)}, u32[]{:S(2)}) copy-start(bf16[288,896]{1,0:T(8,128)(2,1)} %param.21) | copy-start | bytes 1548292
  85.2 53.6 %copy-start.29 = (f32[896]{0:T(1024)S(1)}, f32[896]{0:T(1024)}, u32[]{:S(2)}) copy-start(f32[896]{0:T(1024)} %param.31) | copy-start | bytes 10756
  108.4 30.4 %copy-start.16 = (f32[288,1,7,64]{0,3,2,1:T(8,128)}, f32[288,1,7,64]{0,3,2,1:T(8,128)S(1)}, u32[]{:S(2)}) copy-start(f32[288,1,7,64]{0,3,2,1:T(8,128)S(1)} %get-tuple-element.159) | copy-start | bytes 1548292
  108.4 30.3 %copy-start.23 = (bf16[288,1,7,64]{0,3,2,1:T(8,128)(2,1)}, bf16[288,1,7,64]{0,3,2,1:T(8,128)(2,1)S(1)}, u32[]{:S(2)}) copy-start(bf16[288,1,7,64]{0,3,2,1:T(8,128)(2,1)S(1)} %convert_element_type.125) | copy-start | bytes 774148
  109.8 73.4 %all-reduce.10.cloned.1.call-start = ((), (), s32[]{:S(2)}) async-start(), calls=%async_computation.3 | async-start | bytes 1032192 | tf_op jit(solution)/shard_map/psum | solution.py:186
  151.9 31.3 %copy-start.7 = (bf16[288,896]{1,0:T(8,128)(2,1)S(1)}, bf16[288,896]{1,0:T(8,128)(2,1)}, u32[]{:S(2)}) copy-start(bf16[288,896]{1,0:T(8,128)(2,1)} %all-reduce.8.cloned.1.call-done) | copy-start | bytes 1548292
  154.4 160.6 %reduce-scatter.4.cloned.1.call-start = ((), (), s32[]{:S(2)}) async-start(), calls=%async_computation.4 | async-start | bytes 2506752
  251.8 111.0 %all-reduce.14.cloned.1.call-start = ((), (), s32[]{:S(2)}) async-start(), calls=%async_computation.6 | async-start | bytes 2064384 | tf_op jit(solution)/shard_map/psum | solution.py:167
  275.5 43.8 %copy-start.32 = (f32[288]{0:T(512)S(1)}, f32[288]{0:T(512)}, u32[]{:S(2)}) copy-start(f32[288]{0:T(512)} %copy-done.31) | copy-start | bytes 3460
  275.7 48.3 %copy-start.3 = (bf16[288,896]{1,0:T(8,128)(2,1)S(1)}, bf16[288,896]{1,0:T(8,128)(2,1)}, u32[]{:S(2)}) copy-start(bf16[288,896]{1,0:T(8,128)(2,1)} %param.21) | copy-start | bytes 1548292
  275.7 48.3 %copy-start.30 = (f32[896]{0:T(1024)S(1)}, f32[896]{0:T(1024)}, u32[]{:S(2)}) copy-start(f32[896]{0:T(1024)} %param.23) | copy-start | bytes 10756
  276.9 49.6 %copy-start.8 = (bf16[288,896]{1,0:T(8,128)(2,1)S(1)}, bf16[288,896]{1,0:T(8,128)(2,1)}, u32[]{:S(2)}) copy-start(bf16[288,896]{1,0:T(8,128)(2,1)} %all-reduce.8.cloned.1.call-done) | copy-start | bytes 1548292
  276.9 49.6 %copy-start.15 = (bf16[288,896]{1,0:T(8,128)(2,1)S(1)}, bf16[288,896]{1,0:T(8,128)(2,1)}, u32[]{:S(2)}) copy-start(bf16[288,896]{1,0:T(8,128)(2,1)} %all-reduce.10.cloned.1.call-done) | copy-start | bytes 1548292
  323.7 564.0 %all-reduce.12.cloned.1.call-start = ((), (), s32[]{:S(2)}) async-start(), calls=%async_computation.5 | async-start | bytes 59637760 | tf_op jit(solution)/shard_map/psum | solution.py:267
  331.2 33.1 %copy-start.38 = (f32[896]{0:T(1024)S(1)}, f32[896]{0:T(1024)}, u32[]{:S(2)}) copy-start(f32[896]{0:T(1024)} %get-tuple-element.299) | copy-start | bytes 10756
  331.2 97.4 %copy-start.36 = (f32[288]{0:T(512)S(1)}, f32[288]{0:T(512)}, u32[]{:S(2)}) copy-start(f32[288]{0:T(512)} %copy-done.35) | copy-start | bytes 3460
  895.0 13.0 %slice-start = ((s8[8716288]{0:T(1024)(128)(4,1)}), s8[4194304]{0:T(1024)(128)(4,1)S(1)}, s32[]{:S(2)}) async-start(s8[8716288]{0:T(1024)(128)(4,1)} %bitcast.287), calls=%async_computation.7 | async-start | bytes 8388608
  895.0 14.6 %slice-start.1 = ((s8[8716288]{0:T(1024)(128)(4,1)}), s8[4194304]{0:T(1024)(128)(4,1)S(1)}, s32[]{:S(2)}) async-start(s8[8716288]{0:T(1024)(128)(4,1)} %bitcast.287), calls=%async_computation.8 | async-start | bytes 8388608
  (37 other events, 162.3 us)
Sparse Core Ops, SparseCore 0:
  13.6 41.0 all-gather.1
  109.9 27.3 all-reduce.7
  154.5 28.5 all-reduce.9
  251.9 63.1 reduce-scatter.3
  323.9 38.8 all-reduce.13
  370.6 517.1 all-reduce.11
where the time goes:
time: 930 us; the launch traced here: 920 us
  waiting for transfers between devices  618 us (66%)
  matrix products  136 us (15%)
  blocking collectives  64.3 us (7%)
  local copies, waits for them, and re-layouts  45.5 us (5%)
  other arithmetic  33.9 us (4%)
  between operations  15 us (2%)
    psum x1, waiting for transfers between devices, per_device(): lax.psum((attn_gain_grad, query_grad, query_bias_grad, key_grad, key_bias...  456 us
    psum x1, blocking collectives, per_device(): lax.psum((attn_gain_grad, query_grad, query_bias_grad, key_grad, key_bias...  64.3 us
    unnamed x7, waiting for transfers between devices  38.2 us
    all_gather x1, waiting for transfers between devices, per_device(): kv_all = lax.all_gather(kv_own, 'seq', axis=0, tiled=True)  37.1 us
    unnamed x102, local copies, waits for them, and re-layouts  31.3 us
    psum x1, waiting for transfers between devices, per_device(): lax.psum(jnp.dot(mixed, down_weight, preferred_element_type=jnp.float32)....  30.6 us
    psum x1, waiting for transfers between devices, per_device(): lax.psum(grad_normed_mlp.astype(jnp.bfloat16), 'tp').astype(jnp.float32)  28.7 us
    psum x1, waiting for transfers between devices, per_device(): lax.psum(jnp.dot(attention_low, out_weight, preferred_element_type=jnp.fl...  27.3 us
  transfers between devices with their start and end apart: 6, of which 6 were waited for; matrix products, arithmetic and copies ran while one was open for 4% of the time, Pallas kernels for 0%

commit v1 on v0

v1 whole, which is shorter than its diff:
```python
import functools

import jax
import jax.numpy as jnp
from jax import lax
from jax.experimental import pallas as pl
from jax.experimental.pallas import tpu as pltpu
from jax.sharding import PartitionSpec as P

HEAD_DIM = 64
EPSILON = 1e-06
NEGATIVE = -1e30
ROPE_BASE = 1000000.0
LANES = 128
QUAD = 4
GRAIN = 8
MESH = pl.DeviceIdType.MESH
VMEM_LIMIT = 60 * 1024 * 1024
BF16 = jnp.bfloat16
F32 = jnp.float32


def round_up(value, step):
    return -(-value // step) * step


def nn(left, right):
    return lax.dot_general(left, right, (((1,), (0,)), ((), ())), preferred_element_type=F32)


def nt(left, right):
    return lax.dot_general(left, right, (((1,), (1,)), ((), ())), preferred_element_type=F32)


def tn(left, right):
    return lax.dot_general(left, right, (((0,), (0,)), ((), ())), preferred_element_type=F32)


class Place:
    def __init__(self, groups):
        seq = lax.axis_index("seq").astype(jnp.int32)
        tp = lax.axis_index("tp").astype(jnp.int32)
        self.groups = groups
        self.seq = seq
        self.tp = tp
        self.group = seq // QUAD
        self.quad = seq % QUAD
        self.core = seq % 2
        self.side = (seq // 2) % 2
        self.sibling = (seq + 1 - 2 * self.core, tp)
        self.across = (seq + 2 - 4 * self.side, tp)
        self.partner = (seq, 1 - tp)

    def seq_at(self, group, side, core):
        return group * QUAD + side * 2 + core

    def in_group(self, group):
        return (group * QUAD + self.quad, self.tp)


def send(src, dst, send_sem, recv_sem, device):
    pltpu.make_async_remote_copy(
        src_ref=src,
        dst_ref=dst,
        send_sem=send_sem,
        recv_sem=recv_sem,
        device_id=device,
        device_id_type=MESH,
    ).start()


def sent(src, send_sem, device):
    pltpu.make_async_remote_copy(
        src_ref=src,
        dst_ref=src,
        send_sem=send_sem,
        recv_sem=send_sem,
        device_id=device,
        device_id_type=MESH,
    ).wait_send()


def arrived(dst, recv_sem, device):
    pltpu.make_async_remote_copy(
        src_ref=dst,
        dst_ref=dst,
        send_sem=recv_sem,
        recv_sem=recv_sem,
        device_id=device,
        device_id_type=MESH,
    ).wait_recv()


def meet(place, whole_column):
    barrier = pltpu.get_barrier_semaphore()
    for device in (place.sibling, place.across, place.partner):
        pl.semaphore_signal(barrier, inc=1, device_id=device, device_id_type=MESH)
    if whole_column:
        for step in range(1, place.groups):
            other = place.in_group((place.group + step) % place.groups)
            pl.semaphore_signal(barrier, inc=1, device_id=other, device_id_type=MESH)
        pl.semaphore_wait(barrier, 3 + place.groups - 1)
    else:
        pl.semaphore_wait(barrier, 3)


class LayerGather:
    def __init__(self, place, all_ref, half, recv, part, sems):
        self.place = place
        self.all_ref = all_ref
        self.half = half
        self.first = round_up(half // 2, 16)
        self.recv, self.part, self.sems = recv, part, sems

    def index(self, flip_side, flip_core, flip_tp):
        place = self.place
        side = 1 - place.side if flip_side else place.side
        core = 1 - place.core if flip_core else place.core
        tp = 1 - place.tp if flip_tp else place.tp
        return (side * 2 + core) * 2 + tp

    def rows(self, block, start=0, size=None):
        size = self.half if size is None else size
        return self.all_ref.at[pl.ds(pl.multiple_of(block * self.half + start, 16), size)]

    def start(self):
        place = self.place
        own = self.index(0, 0, 0)
        for number, device in enumerate((place.across, place.partner, place.sibling)):
            send(self.rows(own), self.rows(own), self.sems.at[number], self.recv.at[own], device)

    def from_across(self):
        place = self.place
        block = self.index(1, 0, 0)
        arrived(self.rows(block), self.recv.at[block], place.across)
        part = self.rows(block, 0, self.first)
        send(part, part, self.sems.at[3], self.part.at[0], place.partner)
        send(self.rows(block), self.rows(block), self.sems.at[4], self.recv.at[block], place.sibling)

    def from_partner(self):
        place = self.place
        block = self.index(0, 0, 1)
        arrived(self.rows(block), self.recv.at[block], place.partner)
        part = self.rows(block, self.first, self.half - self.first)
        send(part, part, self.sems.at[5], self.part.at[1], place.across)
        send(self.rows(block), self.rows(block), self.sems.at[6], self.recv.at[block], place.sibling)

    def diagonal(self):
        place = self.place
        block = self.index(1, 0, 1)
        arrived(self.rows(block, 0, self.first), self.part.at[0], place.partner)
        arrived(self.rows(block, self.first, self.half - self.first), self.part.at[1], place.across)
        send(self.rows(block), self.rows(block), self.sems.at[7], self.recv.at[block], place.sibling)

    def finish(self):
        place = self.place
        for side in (0, 1):
            for tp in (0, 1):
                block = self.index(side, 1, tp)
                arrived(self.rows(block), self.recv.at[block], place.sibling)
        own = self.index(0, 0, 0)
        for number, device in enumerate((place.across, place.partner, place.sibling)):
            sent(self.rows(own), self.sems.at[number], device)
        sent(self.rows(own, 0, self.first), self.sems.at[3], place.partner)
        sent(self.rows(own), self.sems.at[4], place.sibling)
        sent(self.rows(own, self.first, self.half - self.first), self.sems.at[5], place.across)
        sent(self.rows(own), self.sems.at[6], place.sibling)
        sent(self.rows(own), self.sems.at[7], place.sibling)


def extended_keys(kv, chip, rows, width, slots):
    count = kv.shape[0]
    lane = lax.broadcasted_iota(jnp.int32, (count, width), 1) - HEAD_DIM
    row = lax.broadcasted_iota(jnp.int32, (count, width), 0)
    block = rows // 2
    number = jnp.zeros_like(row)
    for edge in range(block, count, block):
        number = number + (row >= edge).astype(jnp.int32)
    hot = (lane == number + chip * (count // block)) | ((lane >= slots) & (lane < slots + 3))
    extra = jnp.where(hot, 1.0, 0.0).astype(BF16)
    if width == LANES:
        return jnp.where(lane < 0, kv, extra)
    first = jnp.where(lane[:, :LANES] < 0, kv, extra[:, :LANES])
    return jnp.concatenate([first, extra[:, LANES:]], axis=1)


def hide_later(scores, place, rows, first_query):
    count, width = scores.shape
    block = rows // 2
    key = lax.broadcasted_iota(jnp.int32, (count, 1), 0) - place.core * rows
    query = lax.broadcasted_iota(jnp.int32, (1, width), 1) + first_query
    query = query % rows
    end = jnp.where(query < block, block, rows)
    return jnp.where((key > query) & (key < end), NEGATIVE, scores)


def split_rows(values, at, count):
    one = values.astype(BF16).astype(F32)
    two = (values - one).astype(BF16).astype(F32)
    three = values - one - two
    row = lax.broadcasted_iota(jnp.int32, (count, values.shape[1]), 0) - at
    picked = jnp.where(row == 0, one, jnp.where(row == 1, two, jnp.where(row == 2, three, 0.0)))
    return picked.astype(BF16)


def attend_kernel(
    groups,
    slots,
    kv_own,
    qt,
    x_in,
    out_weight,
    gain,
    cot,
    kv_all,
    normed_all,
    cot_all,
    resid_out,
    att_out,
    ot_out,
    lse_out,
    s_buf,
    m_buf,
    l_buf,
    part_buf,
    part_send,
    part_recv,
    kv_recv,
    kv_z,
    kv_x,
    kv_sib,
    n_recv,
    n_part,
    n_sems,
    c_recv,
    c_part,
    c_sems,
    p_sems,
):
    place = Place(groups)
    rows = kv_own.shape[0]
    half = rows // 2
    span = 2 * rows
    width, queries = qt.shape
    block = queries // 2
    chunks = 2 * groups
    heads = out_weight.shape[0] // HEAD_DIM

    kv_all[pl.ds(place.seq * rows, rows), :] = kv_own[...]
    own_half = place.quad * 2 + place.tp
    cot_all[pl.ds(pl.multiple_of(own_half * half, 16), half), :] = cot[
        pl.ds(pl.multiple_of(place.tp * half, 16), half), :
    ]
    meet(place, True)

    def kv_rows(seq):
        return kv_all.at[pl.ds(pl.multiple_of(seq * rows, 16), rows)]

    own = kv_rows(place.seq)
    send(own, own, kv_sib.at[0], kv_recv.at[place.seq], place.sibling)
    for step in range(1, groups):
        other = place.in_group((place.group + step) % groups)
        send(own, own, kv_z.at[step - 1], kv_recv.at[place.seq], other)
    send(own, own, kv_x.at[0], kv_recv.at[place.seq], place.across)

    def chunk_place(number):
        far = number % 2
        group = (place.group + number // 2) % groups
        side = place.side + far * (1 - 2 * place.side)
        return group, side

    def pass_on(number):
        group, side = chunk_place(number)
        seq = place.seq_at(group, side, place.core)
        view = kv_rows(seq)
        arrived(view, kv_recv.at[seq], place.across)
        send(view, view, kv_sib.at[number], kv_recv.at[seq], place.sibling)

        @pl.when(number % 2 == 0)
        def near():
            send(view, view, kv_x.at[number // 2], kv_recv.at[seq], place.across)

    def ready(number):
        group, side = chunk_place(number)
        seq = place.seq_at(group, side, 1 - place.core)
        arrived(kv_rows(seq), kv_recv.at[seq], place.sibling)

    gather_cot = LayerGather(place, cot_all, half, c_recv, c_part, c_sems)
    gather_normed = LayerGather(place, normed_all, half, n_recv, n_part, n_sems)

    def kv_chunk(number):
        group, side = chunk_place(number)
        chip = group * 2 + side
        return chip, kv_all[pl.ds(pl.multiple_of(chip * span, 16), span), :]

    def scores(number, part, slot, own_chip=False):
        chip, kv = kv_chunk(number)
        keys = extended_keys(kv, chip, rows, width, slots)
        value = nn(keys, qt[:, part * block : (part + 1) * block])
        if own_chip:
            value = hide_later(value, place, rows, part * block)
        s_buf[slot] = value

    def absorb(number, part, slot, first=False):
        chip, kv = kv_chunk(number)
        lanes = slice(part * block, (part + 1) * block)
        value = s_buf[slot]
        top = jnp.max(value, axis=0, keepdims=True)
        if not first:
            old = m_buf[:, lanes]
            top = jnp.maximum(old, top)
            shrink = jnp.exp(old - top)
        weights = jnp.exp(value - top)
        total = jnp.sum(weights, axis=0, keepdims=True)
        product = tn(kv[:, HEAD_DIM:], weights.astype(BF16))
        if not first:
            total = total + l_buf[:, lanes] * shrink
            product = product + ot_out[:, lanes] * shrink
        m_buf[:, lanes] = top
        l_buf[:, lanes] = total
        ot_out[:, lanes] = product

    ready(0)
    scores(0, 0, 0, True)
    scores(0, 1, 1, True)
    absorb(0, 0, 0, True)
    pass_on(1)
    pass_on(2)
    ready(1)
    scores(1, 0, 0)
    absorb(0, 1, 1, True)

    def step(number, unused):
        scores(number, 1, 1)
        absorb(number, 0, 0)

        @pl.when(number + 2 < chunks)
        def look_ahead():
            pass_on(number + 2)

        @pl.when(number + 1 < chunks)
        def next_ready():
            ready(number + 1)

        @pl.when(number == 1)
        def cot_start():
            gather_cot.start()

        @pl.when(number == chunks - 3)
        def cot_middle():
            gather_cot.from_across()
            gather_cot.from_partner()

        scores(jnp.minimum(number + 1, chunks - 1), 0, 0)
        absorb(number, 1, 1)
        return unused

    lax.fori_loop(1, chunks, step, 0)

    ot = ot_out[...] / l_buf[...]
    ot_out[...] = ot
    lse_out[...] = m_buf[...] + jnp.log(l_buf[...])
    natural = jnp.transpose(ot).astype(BF16)
    att = jnp.concatenate(
        [natural[head * rows : (head + 1) * rows, :] for head in range(heads)], axis=1
    )
    att_out[...] = att
    part_buf[...] = nn(att, out_weight[...])
    other_rows = pl.ds(pl.multiple_of((1 - place.tp) * half, 16), half)
    my_rows = pl.ds(pl.multiple_of(place.tp * half, 16), half)
    part_send[...] = part_buf[other_rows, :].astype(BF16)
    send(part_send, part_recv, p_sems.at[0], p_sems.at[1], place.partner)
    gather_cot.diagonal()
    mine = part_buf[my_rows, :] + x_in[my_rows, :].astype(F32)
    arrived(part_recv, p_sems.at[1], place.partner)
    resid = mine + part_recv[...].astype(F32)
    resid_out[...] = resid
    factor = lax.rsqrt(jnp.mean(resid * resid, axis=-1, keepdims=True) + EPSILON)
    normed_all[pl.ds(pl.multiple_of(own_half * half, 16), half), :] = (
        resid * factor * gain[...]
    ).astype(BF16)
    gather_normed.start()
    gather_normed.from_across()
    gather_normed.from_partner()
    gather_normed.diagonal()
    gather_normed.finish()
    gather_cot.finish()
    sent(part_send, p_sems.at[0], place.partner)

    def close(number, unused):
        sent(own, kv_sib.at[number], place.sibling)
        return unused

    lax.fori_loop(0, chunks, close, 0)
    for step_out in range(groups):
        sent(own, kv_x.at[step_out], place.across)
    for step_out in range(1, groups):
        sent(own, kv_z.at[step_out - 1], place.in_group((place.group + step_out) % groups))


class ChainSum:
    def __init__(self, place, own, incoming, final, sems):
        self.place = place
        self.own, self.incoming, self.final = own, incoming, final
        self.count = own.shape[0]
        (
            self.up_recv,
            self.up_send,
            self.fin_recv,
            self.fin_send,
            self.x_recv,
            self.x_send,
            self.c_recv,
            self.c_send,
        ) = sems

    def root(self, parity):
        return self.place.groups // 2 - 1 + parity

    def lag_up(self, parity):
        groups, group, root = self.place.groups, self.place.group, self.root(parity)
        most = max(root, groups - 1 - root)
        return jnp.where(
            group < root, group, jnp.where(group > root, groups - 1 - group, most)
        )

    def lag_down(self, parity):
        groups, group, root = self.place.groups, self.place.group, self.root(parity)
        most = max(root, groups - 1 - root)
        return most + jnp.abs(group - root)

    def total_steps(self):
        groups = self.place.groups
        most = groups // 2
        return self.count + 2 * most + 2

    def spread(self, i):
        place = self.place
        view = self.final.at[place.quad, i]
        send(view, view, self.x_send.at[i], self.x_recv.at[i], place.across)
        send(view, view, self.c_send.at[0, i], self.c_recv.at[0, i], place.sibling)

    def up(self, i, parity):
        place, root = self.place, self.root(parity)
        group, last = place.group, place.groups - 1
        mine = self.own.at[i]

        @pl.when((group > 0) & (group <= root))
        def from_left():
            arrived(self.incoming.at[i], self.up_recv.at[0, i], place.in_group(group - 1))
            mine[...] = (mine[...].astype(F32) + self.incoming[i].astype(F32)).astype(BF16)

        @pl.when((group < last) & (group > root))
        def from_right():
            arrived(self.incoming.at[i], self.up_recv.at[1, i], place.in_group(group + 1))
            mine[...] = (mine[...].astype(F32) + self.incoming[i].astype(F32)).astype(BF16)

        @pl.when(group < root)
        def to_right():
            send(
                mine,
                self.incoming.at[i],
                self.up_send.at[i],
                self.up_recv.at[0, i],
                place.in_group(group + 1),
            )

        @pl.when(group > root + 1)
        def to_left():
            send(
                mine,
                self.incoming.at[i],
                self.up_send.at[i],
                self.up_recv.at[1, i],
                place.in_group(group - 1),
            )

        @pl.when(group == root + 1)
        def to_root():
            send(
                mine,
                self.final.at[place.quad, i],
                self.up_send.at[i],
                self.up_recv.at[1, i],
                place.in_group(group - 1),
            )

        @pl.when(group == root)
        def at_root():
            view = self.final.at[place.quad, i]

            @pl.when(group < last)
            def both():
                arrived(view, self.up_recv.at[1, i], place.in_group(group + 1))
                view[...] = (mine[...].astype(F32) + view[...].astype(F32)).astype(BF16)

            @pl.when(group == last)
            def alone():
                view[...] = mine[...]

            @pl.when(group > 0)
            def left():
                send(
                    view,
                    view,
                    self.fin_send.at[0, i],
                    self.fin_recv.at[i],
                    place.in_group(group - 1),
                )

            @pl.when(group < last)
            def right():
                send(
                    view,
                    view,
                    self.fin_send.at[1, i],
                    self.fin_recv.at[i],
                    place.in_group(group + 1),
                )

            self.spread(i)

    def down(self, i, parity):
        place, root = self.place, self.root(parity)
        group, last = place.group, place.groups - 1
        view = self.final.at[place.quad, i]

        @pl.when(group != root)
        def take():
            arrived(view, self.fin_recv.at[i], place.sibling)

            @pl.when((group < root) & (group > 0))
            def left():
                send(
                    view,
                    view,
                    self.fin_send.at[0, i],
                    self.fin_recv.at[i],
                    place.in_group(group - 1),
                )

            @pl.when((group > root) & (group < last))
            def right():
                send(
                    view,
                    view,
                    self.fin_send.at[1, i],
                    self.fin_recv.at[i],
                    place.in_group(group + 1),
                )

            self.spread(i)

    def cross(self, i):
        place = self.place
        view = self.final.at[place.across[0] % QUAD, i]
        arrived(view, self.x_recv.at[i], place.across)
        send(view, view, self.c_send.at[1, i], self.c_recv.at[1, i], place.sibling)

    def step(self, number):
        for parity in (0, 1):
            i = number - self.lag_up(parity)

            @pl.when((i >= 0) & (i < self.count) & (i % 2 == parity))
            def go_up(i=i, parity=parity):
                self.up(i, parity)

        for parity in (0, 1):
            i = number - self.lag_down(parity)

            @pl.when((i >= 0) & (i < self.count) & (i % 2 == parity))
            def go_down(i=i, parity=parity):
                self.down(i, parity)

        for parity in (0, 1):
            i = number - self.lag_down(parity) - 1

            @pl.when((i >= 0) & (i < self.count) & (i % 2 == parity))
            def go_cross(i=i):
                self.cross(i)

    def finish(self):
        place = self.place
        group, last = place.group, place.groups - 1
        sibling_quad = place.sibling[0] % QUAD
        diagonal = 3 - place.quad

        def close(i, unused):
            root = place.groups // 2 - 1 + i % 2
            view = self.own.at[i]
            arrived(self.final.at[sibling_quad, i], self.c_recv.at[0, i], place.sibling)
            arrived(self.final.at[diagonal, i], self.c_recv.at[1, i], place.sibling)

            @pl.when(group != root)
            def up_done():
                sent(view, self.up_send.at[i], place.sibling)

            @pl.when((group <= root) & (group > 0))
            def left_done():
                sent(view, self.fin_send.at[0, i], place.sibling)

            @pl.when((group >= root) & (group < last))
            def right_done():
                sent(view, self.fin_send.at[1, i], place.sibling)

            sent(view, self.x_send.at[i], place.across)
            sent(view, self.c_send.at[0, i], place.sibling)
            sent(view, self.c_send.at[1, i], place.sibling)
            return unused

        lax.fori_loop(0, self.count, close, 0)


def chain_sems(count):
    dma = pltpu.SemaphoreType.DMA
    return [
        dma((2, count)),
        dma((count,)),
        dma((count,)),
        dma((2, count)),
        dma((count,)),
        dma((count,)),
        dma((2, count)),
        dma((2, count)),
    ]


class LayerSum:
    def __init__(self, place, part, half, core_in, left, right, left_in, right_in, last_in, sems):
        self.place, self.part, self.half = place, part, half
        self.core_in, self.left, self.right = core_in, left, right
        self.left_in, self.right_in, self.last_in = left_in, right_in, last_in
        self.sems = sems
        self.cut = left.shape[2]
        self.columns = part.shape[1]

    def rows(self, side, core):
        size = 2 * self.half
        return pl.ds(pl.multiple_of((side * 2 + core) * size, 16), size)

    def start(self):
        place = self.place
        for side in (0, 1):
            view = self.part.at[self.rows(side, 1 - place.core)]
            send(
                view,
                self.core_in.at[side],
                self.sems.at[side],
                self.sems.at[2 + side],
                place.sibling,
            )

    def own_rows(self, tp):
        return pl.ds(pl.multiple_of(tp * self.half, 16), self.half)

    def after_core(self):
        place = self.place
        for side in (0, 1):
            arrived(self.core_in.at[side], self.sems.at[2 + side], place.sibling)
            total = self.part[self.rows(side, place.core), :].astype(F32) + self.core_in[
                side
            ].astype(F32)
            self.left[side] = total[:, : self.cut].astype(BF16)
            self.right[side] = total[:, self.cut :].astype(BF16)

    def cross(self):
        place = self.place
        for side in (0, 1):
            send(
                self.left.at[side, self.own_rows(1 - place.tp)],
                self.left_in.at[side],
                self.sems.at[4 + side],
                self.sems.at[6 + side],
                place.partner,
            )
        send(
            self.right.at[1 - place.side],
            self.right_in,
            self.sems.at[8],
            self.sems.at[9],
            place.across,
        )

    def after_cross(self):
        place = self.place
        mine = self.own_rows(place.tp)
        for side in (0, 1):
            arrived(self.left_in.at[side], self.sems.at[6 + side], place.partner)
            self.left_in[side] = (
                self.left[side, mine, :].astype(F32) + self.left_in[side].astype(F32)
            ).astype(BF16)
        arrived(self.right_in, self.sems.at[9], place.across)
        self.right_in[...] = (
            self.right[place.side].astype(F32) + self.right_in[...].astype(F32)
        ).astype(BF16)
        send(
            self.left_in.at[1 - place.side],
            self.last_in.at[:, : self.cut],
            self.sems.at[10],
            self.sems.at[11],
            place.across,
        )
        send(
            self.right_in.at[self.own_rows(1 - place.tp)],
            self.last_in.at[:, self.cut :],
            self.sems.at[12],
            self.sems.at[13],
            place.partner,
        )

    def result(self):
        place = self.place
        arrived(self.last_in.at[:, : self.cut], self.sems.at[11], place.across)
        arrived(self.last_in.at[:, self.cut :], self.sems.at[13], place.partner)
        mine = jnp.concatenate(
            [self.left_in[place.side], self.right_in[self.own_rows(place.tp), :]], axis=1
        )
        return mine.astype(F32) + self.last_in[...].astype(F32)

    def finish(self):
        place = self.place
        for side in (0, 1):
            sent(self.core_in.at[side], self.sems.at[side], place.sibling)
            sent(self.left_in.at[side], self.sems.at[4 + side], place.partner)
        sent(self.right_in, self.sems.at[8], place.across)
        sent(self.last_in.at[:, : self.cut], self.sems.at[10], place.across)
        sent(self.last_in.at[:, self.cut :], self.sems.at[12], place.partner)


def layer_sum_scratch(half, columns):
    cut = columns // LANES // 2 * LANES
    if cut * 2 < columns:
        cut += LANES
    return [
        pltpu.VMEM((2, 2 * half, columns), BF16),
        pltpu.VMEM((2, 2 * half, cut), BF16),
        pltpu.VMEM((2, 2 * half, columns - cut), BF16),
        pltpu.VMEM((2, half, cut), BF16),
        pltpu.VMEM((2 * half, columns - cut), BF16),
        pltpu.VMEM((half, columns), BF16),
        pltpu.SemaphoreType.DMA((14,)),
    ]


def backward_kernel(
    groups,
    slots,
    grad_part,
    mlp_part,
    wide_in,
    tall_in,
    resid_in,
    cot,
    gain,
    out_weight,
    att,
    ot,
    lse,
    qt_in,
    kv_all,
    layer_out,
    resid_grad,
    dq_out,
    dkv_out,
    wide,
    tall,
    out_grad,
    gain_grad,
    *scratch,
):
    place = Place(groups)
    wide_own, tall_own, wide_up, tall_up = scratch[0:4]
    wide_sems, tall_sems = scratch[4:12], scratch[12:20]
    sum_g, sum_m = scratch[20:27], scratch[27:34]
    branch, qt, dot_t, q_pad, do_pad, dkv = scratch[34:40]
    sib_send, sib_in, x_send, x_in, z_send, z_in = scratch[40:46]
    kv_sems, pair_sems = scratch[46:48]
    rows = att.shape[0]
    half = rows // 2
    span = 2 * rows
    width, queries = qt_in.shape
    block = queries // 2
    chunks = 2 * groups
    heads = out_weight.shape[0] // HEAD_DIM
    my_rows = pl.ds(pl.multiple_of(place.tp * half, 16), half)
    other_rows = pl.ds(pl.multiple_of((1 - place.tp) * half, 16), half)

    grad_sum = LayerSum(place, grad_part, half, *sum_g)
    mlp_sum = LayerSum(place, mlp_part, half, *sum_m)
    tall_sum = ChainSum(place, tall_own, tall_up, tall, tall_sems)
    wide_sum = ChainSum(place, wide_own, wide_up, wide, wide_sems)
    fills = [
        pltpu.make_async_copy(tall_in, tall_own, pair_sems.at[4]),
        pltpu.make_async_copy(wide_in, wide_own, pair_sems.at[5]),
    ]
    for fill in fills:
        fill.start()
    tall_steps = tall_sum.count

    def chain_step(number):
        tall_sum.step(number)
        wide_sum.step(number - tall_steps)

    all_steps = tall_steps + wide_sum.total_steps()

    meet(place, True)
    grad_sum.start()
    for fill in fills:
        fill.wait()
    chain_step(0)
    mlp_sum.start()

    qt[...] = qt_in[...]
    at = HEAD_DIM + slots
    qt[at : at + 16, :] = split_rows(-lse[...], 0, 16)
    natural_q = jnp.transpose(qt_in[0:HEAD_DIM, :].astype(F32)).astype(BF16)
    q_pad[...] = jnp.concatenate([natural_q, jnp.zeros_like(natural_q)], axis=1)

    grad_sum.after_core()
    grad_sum.cross()
    chain_step(1)
    mlp_sum.after_core()
    grad_sum.after_cross()
    mlp_sum.cross()
    chain_step(2)

    resid = resid_in[...]
    factor = lax.rsqrt(jnp.mean(resid * resid, axis=-1, keepdims=True) + EPSILON)
    normed = resid * factor
    grad_normed = grad_sum.result()
    gain_grad[...] = jnp.sum(grad_normed * normed, axis=0, keepdims=True)
    weighted = grad_normed * gain[...]
    inner = jnp.mean(weighted * normed, axis=-1, keepdims=True)
    grad_resid = cot[my_rows, :].astype(F32) + factor * (weighted - normed * inner)
    resid_grad[...] = grad_resid
    branch[my_rows, :] = grad_resid.astype(BF16)
    send(
        branch.at[my_rows],
        branch.at[my_rows],
        pair_sems.at[0],
        pair_sems.at[1],
        place.partner,
    )
    mlp_sum.after_cross()
    chain_step(3)
    chain_step(4)
    arrived(branch.at[other_rows], pair_sems.at[1], place.partner)

    grads = branch[...]
    out_grad[...] = tn(att[...], grads)
    grad_att = nt(grads, out_weight[...]).astype(BF16)
    stacked = jnp.concatenate(
        [grad_att[:, head * HEAD_DIM : (head + 1) * HEAD_DIM] for head in range(heads)]
        + [jnp.zeros((queries - heads * rows, HEAD_DIM), BF16)],
        axis=0,
    )
    do_pad[...] = jnp.concatenate([jnp.zeros_like(stacked), stacked], axis=1)
    turned = jnp.transpose(stacked.astype(F32))
    delta = jnp.sum(turned * ot[...], axis=0, keepdims=True)
    dot_t[0:HEAD_DIM, :] = split_rows(-delta, 0, HEAD_DIM)
    dot_t[HEAD_DIM:, :] = turned.astype(BF16)
    chain_step(5)
    layer_out[my_rows, :] = (resid + mlp_sum.result()).astype(BF16)
    send(
        layer_out.at[my_rows],
        layer_out.at[my_rows],
        pair_sems.at[2],
        pair_sems.at[3],
        place.partner,
    )
    dq_out[...] = jnp.zeros_like(dq_out)

    def chunk_place(number):
        far = 1 - number % 2
        group = (place.group + 1 + number // 2) % groups
        side = place.side + far * (1 - 2 * place.side)
        return group, side

    lane = lax.broadcasted_iota(jnp.int32, (1, LANES), 1)
    ones = jnp.where(lane < 3, 1.0, 0.0).astype(BF16)

    def attend_back(number, slot, own_chip=False):
        group, side = chunk_place(number)
        chip = group * 2 + side
        at_rows = pl.ds(pl.multiple_of(chip * span, 16), span)
        kv = kv_all[at_rows, :]
        keys = extended_keys(kv, chip, rows, width, slots)
        values = jnp.where(lane >= HEAD_DIM, kv, jnp.broadcast_to(ones, kv.shape))
        for part in range(2):
            lanes = slice(part * block, (part + 1) * block)
            score = nn(keys, qt[:, lanes])
            if own_chip:
                score = hide_later(score, place, rows, part * block)
            weights = jnp.exp(score)
            change = nn(values, dot_t[:, lanes])
            low = (weights * change).astype(BF16)
            total = nn(weights.astype(BF16), do_pad[lanes, :]) + nn(low, q_pad[lanes, :])
            if part == 0:
                dkv[slot] = total
            else:
                dkv[slot] += total
            dq_out[:, lanes] += tn(kv[:, :HEAD_DIM], low)

    def hand_over(number, slot):
        other = pl.ds(pl.multiple_of((1 - place.core) * rows, 16), rows)
        sib_send[number] = dkv[slot, other, :].astype(BF16)
        send(
            sib_send.at[number],
            sib_in.at[number],
            kv_sems.at[0, number],
            kv_sems.at[1, number],
            place.sibling,
        )

    def take_over(number, near, own_group=False):
        group, side = chunk_place(number)
        step = number // 2
        arrived(sib_in.at[number], kv_sems.at[1, number], place.sibling)
        mine = pl.ds(pl.multiple_of(place.core * rows, 16), rows)
        total = dkv[1 if near else 0, mine, :] + sib_in[number].astype(F32)
        if not near:
            x_send[step] = total.astype(BF16)
            send(
                x_send.at[step],
                x_in.at[step],
                kv_sems.at[2, step],
                kv_sems.at[3, step],
                place.across,
            )
            return
        arrived(x_in.at[step], kv_sems.at[3, step], place.across)
        total = total + x_in[step].astype(F32)
        if own_group:
            dkv_out[...] = total
            return
        z_send[step] = total.astype(BF16)
        back = groups - 2 - step
        send(
            z_send.at[step],
            z_in.at[back],
            kv_sems.at[4, step],
            kv_sems.at[5, back],
            place.in_group(group),
        )

    def pair(step, unused):
        attend_back(2 * step, 0)
        hand_over(2 * step, 0)
        chain_step(6 + 2 * step)

        @pl.when(step > 0)
        def last_near():
            take_over(2 * step - 1, True)

        attend_back(2 * step + 1, 1)
        hand_over(2 * step + 1, 1)
        take_over(2 * step, False)
        chain_step(7 + 2 * step)
        return unused

    lax.fori_loop(0, groups - 1, pair, 0)
    attend_back(chunks - 2, 0)
    hand_over(chunks - 2, 0)
    chain_step(6 + 2 * (groups - 1))
    if groups > 1:
        take_over(chunks - 3, True)
    attend_back(chunks - 1, 1, True)
    hand_over(chunks - 1, 1)
    take_over(chunks - 2, False)
    chain_step(7 + 2 * (groups - 1))
    take_over(chunks - 1, True, True)
    for step in range(groups - 1):
        arrived(z_in.at[step], kv_sems.at[5, step], place.sibling)
        dkv_out[...] += z_in[step].astype(F32)

    def rest(number, unused):
        chain_step(number)
        return unused

    lax.fori_loop(8 + 2 * (groups - 1), all_steps, rest, 0)

    arrived(layer_out.at[other_rows], pair_sems.at[3], place.partner)
    sent(branch.at[my_rows], pair_sems.at[0], place.partner)
    sent(branch.at[my_rows], pair_sems.at[2], place.partner)
    grad_sum.finish()
    mlp_sum.finish()
    tall_sum.finish()
    wide_sum.finish()
    for number in range(chunks):
        sent(sib_send.at[number], kv_sems.at[0, number], place.sibling)
    for step in range(groups):
        sent(x_send.at[step], kv_sems.at[2, step], place.across)
    for step in range(groups - 1):
        sent(z_send.at[step], kv_sems.at[4, step], place.sibling)


def vmem_specs(count):
    return [pl.BlockSpec(memory_space=pltpu.VMEM)] * count


def params(collective):
    return pltpu.CompilerParams(
        collective_id=collective, has_side_effects=True, vmem_limit_bytes=VMEM_LIMIT
    )


def attend(groups, slots, kv_own, qt, x_in, out_weight, gain, cot):
    rows, features = x_in.shape
    half = rows // 2
    total = groups * QUAD * rows
    width, queries = qt.shape
    dma = pltpu.SemaphoreType.DMA
    shape = jax.ShapeDtypeStruct
    return pl.pallas_call(
        functools.partial(attend_kernel, groups, slots),
        out_shape=[
            shape((total, LANES), BF16),
            shape((QUAD * rows, features), BF16),
            shape((QUAD * rows, features), BF16),
            shape((half, features), F32),
            shape((rows, out_weight.shape[0]), BF16),
            shape((HEAD_DIM, queries), F32),
            shape((1, queries), F32),
        ],
        in_specs=vmem_specs(6),
        out_specs=vmem_specs(7),
        scratch_shapes=[
            pltpu.VMEM((2, 2 * rows, queries // 2), F32),
            pltpu.VMEM((1, queries), F32),
            pltpu.VMEM((1, queries), F32),
            pltpu.VMEM((rows, features), F32),
            pltpu.VMEM((half, features), BF16),
            pltpu.VMEM((half, features), BF16),
            dma((groups * QUAD,)),
            dma((groups,)),
            dma((groups,)),
            dma((2 * groups,)),
            dma((8,)),
            dma((2,)),
            dma((8,)),
            dma((8,)),
            dma((2,)),
            dma((8,)),
            dma((2,)),
        ],
        compiler_params=params(1),
        name="attend",
    )(kv_own, qt, x_in, out_weight, gain, cot)


def backward(groups, slots, grad_part, mlp_part, wide, tall, resid, cot, gain, out_weight, att, ot, lse, qt, kv_all):
    rows, inner = att.shape
    half = rows // 2
    features = grad_part.shape[1]
    total = kv_all.shape[0]
    width, queries = qt.shape
    chunks = 2 * groups
    dma = pltpu.SemaphoreType.DMA
    shape = jax.ShapeDtypeStruct
    pass_shape = (rows, LANES)
    return pl.pallas_call(
        functools.partial(backward_kernel, groups, slots),
        out_shape=[
            shape((rows, features), BF16),
            shape((half, features), F32),
            shape((HEAD_DIM, queries), F32),
            shape((rows, LANES), F32),
            shape((QUAD, *wide.shape), BF16),
            shape((QUAD, *tall.shape), BF16),
            shape((inner, features), F32),
            shape((1, features), F32),
        ],
        in_specs=vmem_specs(2) + [pl.BlockSpec(memory_space=pl.ANY)] * 2 + vmem_specs(9),
        out_specs=vmem_specs(8),
        scratch_shapes=[
            pltpu.VMEM(wide.shape, BF16),
            pltpu.VMEM(tall.shape, BF16),
            pltpu.VMEM(wide.shape, BF16),
            pltpu.VMEM(tall.shape, BF16),
            *chain_sems(wide.shape[0]),
            *chain_sems(tall.shape[0]),
            *layer_sum_scratch(half, features),
            *layer_sum_scratch(half, features),
            pltpu.VMEM((rows, features), BF16),
            pltpu.VMEM((width, queries), BF16),
            pltpu.VMEM((LANES, queries), BF16),
            pltpu.VMEM((queries, LANES), BF16),
            pltpu.VMEM((queries, LANES), BF16),
            pltpu.VMEM((2, 2 * rows, LANES), F32),
            pltpu.VMEM((chunks, *pass_shape), BF16),
            pltpu.VMEM((chunks, *pass_shape), BF16),
            pltpu.VMEM((groups, *pass_shape), BF16),
            pltpu.VMEM((groups, *pass_shape), BF16),
            pltpu.VMEM((groups, *pass_shape), BF16),
            pltpu.VMEM((groups, *pass_shape), BF16),
            dma((6, chunks)),
            dma((6,)),
        ],
        compiler_params=params(2),
        name="backward",
    )(grad_part, mlp_part, wide, tall, resid, cot, gain, out_weight, att, ot, lse, qt, kv_all)


def rope_tables(positions, head_size):
    half_size = head_size // 2
    exponent = jnp.arange(half_size, dtype=F32) * (2.0 / head_size)
    frequency = jnp.power(ROPE_BASE, -exponent)
    angle = positions.astype(F32)[:, None] * frequency[None, :]
    return (jnp.cos(angle)[:, None, :], jnp.sin(angle)[:, None, :])


def rotate(values, cosine, sine):
    half_size = values.shape[-1] // 2
    first = values[..., :half_size]
    second = values[..., half_size:]
    return jnp.concatenate(
        [first * cosine - second * sine, second * cosine + first * sine], axis=-1
    )


def rms_backward(grad_normed, normed, factor, gain):
    gain_grad = jnp.sum(grad_normed * normed, axis=0)
    weighted = grad_normed * gain
    values_grad = factor * (weighted - normed * jnp.mean(weighted * normed, axis=-1, keepdims=True))
    return (gain_grad, values_grad)


def piece_of(weight, axis, piece, quad):
    pads = [(0, 0, 0), (0, 0, 0)]
    pads[axis] = (0, piece * QUAD - weight.shape[axis], 0)
    padded = lax.pad(weight, jnp.zeros((), weight.dtype), pads)
    return lax.dynamic_slice_in_dim(padded, quad * piece, piece, axis)


def per_device(
    groups,
    layer_input,
    block_order,
    attn_gain,
    query_weight,
    query_bias,
    key_weight,
    key_bias,
    value_weight,
    value_bias,
    out_weight,
    mlp_gain,
    gate_weight,
    up_weight,
    down_weight,
    out_cotangent,
):
    rows, features = layer_input.shape
    block_rows = rows // 2
    slots = block_order.shape[0]
    hidden = gate_weight.shape[1]
    heads = query_weight.shape[1] // HEAD_DIM
    piece = round_up(hidden // LANES, QUAD) // QUAD * LANES
    queries = round_up(heads * rows, 2 * LANES)
    width = round_up(HEAD_DIM + slots + 16, LANES)
    scale = HEAD_DIM ** (-0.5)
    seq_index = lax.axis_index("seq")
    quad = seq_index % QUAD
    tp_index = lax.axis_index("tp")
    own_slots = lax.dynamic_slice_in_dim(block_order, 2 * seq_index, 2)
    steps_in = jnp.arange(block_rows, dtype=jnp.int32)
    own_places = (own_slots[:, None] * block_rows + steps_in[None, :]).reshape(-1)
    cosine, sine = rope_tables(own_places, HEAD_DIM)
    inputs = layer_input.astype(F32)
    factor_first = lax.rsqrt(jnp.mean(inputs * inputs, axis=-1, keepdims=True) + EPSILON)
    normed_first = inputs * factor_first
    normed_attn = (normed_first * attn_gain).astype(BF16)
    query_rows = (
        jnp.dot(normed_attn, query_weight, preferred_element_type=F32) + query_bias
    ).reshape(rows, heads, HEAD_DIM)
    key_rows = (jnp.dot(normed_attn, key_weight, preferred_element_type=F32) + key_bias).reshape(
        rows, 1, HEAD_DIM
    )
    value_rows = (
        jnp.dot(normed_attn, value_weight, preferred_element_type=F32) + value_bias
    ).astype(BF16)
    query_rot = rotate(query_rows, cosine, sine).astype(BF16)
    key_rot = rotate(key_rows, cosine, sine).astype(BF16).reshape(rows, HEAD_DIM)
    kv_own = jnp.concatenate([key_rot, value_rows], axis=1)
    query_t = jnp.transpose(query_rot * jnp.asarray(scale, BF16), (2, 1, 0)).reshape(
        HEAD_DIM, heads * rows
    )
    later = block_order[:, None] > jnp.repeat(own_slots, block_rows)[None, :]
    bias = jnp.tile(jnp.where(later, NEGATIVE, 0.0).astype(BF16), (1, heads))
    qt = jnp.concatenate(
        [query_t, bias, jnp.zeros((width - HEAD_DIM - slots, heads * rows), BF16)], axis=0
    )
    qt = jnp.pad(qt, ((0, 0), (0, queries - heads * rows)))
    gain_row = mlp_gain[None, :]

    kv_all, normed_all, cot_all, resid, att, ot, lse = attend(
        groups, slots, kv_own, qt, layer_input, out_weight, gain_row, out_cotangent
    )

    gate_piece = piece_of(gate_weight, 1, piece, quad)
    up_piece = piece_of(up_weight, 1, piece, quad)
    down_piece = piece_of(down_weight, 0, piece, quad)
    gate = jnp.dot(normed_all, gate_piece, preferred_element_type=F32)
    upward = jnp.dot(normed_all, up_piece, preferred_element_type=F32)
    sigmoid_gate = jax.nn.sigmoid(gate)
    silu_gate = gate * sigmoid_gate
    mixed = (silu_gate * upward).astype(BF16)
    mlp_part = jnp.dot(mixed, down_piece, preferred_element_type=F32).astype(BF16)
    down_grad = jnp.einsum("rf,rd->fd", mixed, cot_all, preferred_element_type=F32).astype(BF16)
    grad_mixed = jnp.einsum("rd,fd->rf", cot_all, down_piece, preferred_element_type=F32)
    grad_gate = (grad_mixed * upward * sigmoid_gate * (1.0 + gate * (1.0 - sigmoid_gate))).astype(
        BF16
    )
    grad_upward = (grad_mixed * silu_gate).astype(BF16)
    gate_grad = jnp.einsum("rd,rf->df", normed_all, grad_gate, preferred_element_type=F32)
    up_grad = jnp.einsum("rd,rf->df", normed_all, grad_upward, preferred_element_type=F32)
    grad_part = (
        jnp.einsum("rf,df->rd", grad_gate, gate_piece, preferred_element_type=F32)
        + jnp.einsum("rf,df->rd", grad_upward, up_piece, preferred_element_type=F32)
    ).astype(BF16)
    wide = jnp.concatenate([gate_grad.astype(BF16), up_grad.astype(BF16)], axis=0).reshape(
        2 * GRAIN, features // GRAIN, piece
    )
    tall = down_grad.reshape(GRAIN, piece // GRAIN, features)

    layer_output, grad_resid_half, dq, dkv, wide_sum, tall_sum, out_grad, mlp_gain_half = backward(
        groups, slots, grad_part, mlp_part, wide, tall, resid, out_cotangent, gain_row, out_weight,
        att, ot, lse, qt, kv_all,
    )

    keep = hidden - (QUAD - 1) * piece
    wide_sum = wide_sum.reshape(QUAD, 2, features, piece)
    tall_sum = tall_sum.reshape(QUAD, piece, features)

    def side_by_side(number):
        parts = [wide_sum[i, number] for i in range(QUAD - 1)] + [
            wide_sum[QUAD - 1, number][:, :keep]
        ]
        return jnp.concatenate(parts, axis=1).astype(F32)

    gate_sum, up_sum = side_by_side(0), side_by_side(1)
    down_sum = tall_sum.reshape(QUAD * piece, features)[:hidden].astype(F32)

    grad_query_rot = jnp.transpose(
        dq[:, : heads * rows].reshape(HEAD_DIM, heads, rows), (2, 1, 0)
    ) * scale
    grad_query = rotate(grad_query_rot, cosine, -sine).reshape(rows, -1).astype(BF16)
    grad_key = (
        rotate(dkv[:, :HEAD_DIM].reshape(rows, 1, HEAD_DIM), cosine, -sine)
        .reshape(rows, HEAD_DIM)
        .astype(BF16)
    )
    grad_value = dkv[:, HEAD_DIM:].astype(BF16)
    query_grad = jnp.einsum("rd,rh->dh", normed_attn, grad_query, preferred_element_type=F32)
    key_grad = jnp.einsum("rd,rh->dh", normed_attn, grad_key, preferred_element_type=F32)
    value_grad = jnp.einsum("rd,rh->dh", normed_attn, grad_value, preferred_element_type=F32)
    query_bias_grad = jnp.sum(grad_query.astype(F32), axis=0)
    key_bias_grad = jnp.sum(grad_key.astype(F32), axis=0)
    value_bias_grad = jnp.sum(grad_value.astype(F32), axis=0)
    grad_normed_attn = (
        jnp.einsum("rh,dh->rd", grad_query, query_weight, preferred_element_type=F32)
        + jnp.einsum("rh,dh->rd", grad_key, key_weight, preferred_element_type=F32)
        + jnp.einsum("rh,dh->rd", grad_value, value_weight, preferred_element_type=F32)
    )
    grad_normed_attn = lax.psum(grad_normed_attn.astype(BF16), "tp").astype(F32)
    attn_gain_grad, grad_input_part = rms_backward(
        grad_normed_attn, normed_first, factor_first, attn_gain
    )
    grad_resid = lax.all_gather(grad_resid_half, "tp", axis=0, tiled=True)
    input_grad = (grad_resid + grad_input_part).astype(BF16)
    mlp_gain_grad = lax.psum(mlp_gain_half[0], ("seq", "tp"))
    small = jnp.concatenate([attn_gain_grad, query_bias_grad, key_bias_grad, value_bias_grad])
    small = lax.psum(small, "seq")
    attn_gain_grad = small[:features]
    query_bias_grad = small[features : features + heads * HEAD_DIM]
    key_bias_grad = small[features + heads * HEAD_DIM : features + (heads + 1) * HEAD_DIM]
    value_bias_grad = small[features + (heads + 1) * HEAD_DIM :]
    query_grad, key_grad, value_grad, out_grad = (
        value.astype(F32)
        for value in lax.psum(
            tuple(v.astype(BF16) for v in (query_grad, key_grad, value_grad, out_grad)), "seq"
        )
    )
    return (
        layer_output,
        input_grad,
        attn_gain_grad,
        query_grad,
        query_bias_grad,
        key_grad,
        key_bias_grad,
        value_grad,
        value_bias_grad,
        out_grad,
        mlp_gain_grad,
        gate_sum,
        up_sum,
        down_sum,
    )


def solution(mesh):
    groups = mesh.shape["seq"] // QUAD
    by_rows, columns, rows, vector, whole = (
        P("seq", None),
        P(None, "tp"),
        P("tp", None),
        P("tp"),
        P(),
    )
    return jax.shard_map(
        functools.partial(per_device, groups),
        mesh=mesh,
        in_specs=(
            by_rows, whole, whole, columns, vector, columns, vector, columns, vector, rows,
            whole, columns, columns, rows, by_rows,
        ),
        out_specs=(
            by_rows, by_rows, whole, columns, vector, columns, vector, columns, vector, rows,
            whole, columns, columns, rows,
        ),
        check_vma=False,
    )
```

time: 930 us -> 430 us (0.46)
  waiting for transfers between devices: 618 us -> 21.7 us
  Pallas kernels: 0 us -> 225 us
  matrix products: 136 us -> 34 us
  local copies, waits for them, and re-layouts: 45.5 us -> 11.9 us
  blocking collectives: 64.3 us -> 88.7 us
    psum x4 -> x2, waiting for transfers between devices: 543 us -> 21.7 us  [the longest x1 21.7 us: per_device(): lax.psum(tuple((v.astype(BF16) for v in (query_grad, key_grad, value_grad...]
    pallas_call x0 -> x2, Pallas kernels: none -> 225 us  [the longest x1 168 us: backward(): pl.pallas_call(functools.partial(backward_kernel, groups, slots), out_sha...]
    dot_general x40 -> x16, matrix products: 133 us -> 32.4 us  [the longest x1 4.09 us: per_device(): upward = jnp.dot(normed_all, up_piece, preferred_element_type=F32)]
    unnamed x7 -> x2, waiting for transfers between devices: 38.2 us -> 0.03 us
    all_gather x1 -> x0, waiting for transfers between devices: 37.1 us -> none  [per_device(): kv_all = lax.all_gather(kv_own, 'seq', axis=0, tiled=True)]
    unnamed x102 -> x63, local copies, waits for them, and re-layouts: 31.3 us -> 2.34 us
    all_gather x0 -> x1, blocking collectives: none -> 18.3 us  [per_device(): grad_resid = lax.all_gather(grad_resid_half, 'tp', axis=0, tiled=True)]
    convert_element_type x4 -> x10, other arithmetic: 4.36 us -> 19 us  [the longest x1 6.53 us: side_by_side(): return jnp.concatenate(parts, axis=1).astype(F32)]
  transfers between devices with their start and end apart: 6 -> 2, of which waited for: 6 -> 1; matrix products, arithmetic and copies ran while one was open for 4% -> 6% of each run, Pallas kernels for 0% -> 0%
where the time goes in v1:
time: 430 us; the launch traced here: 425 us
  Pallas kernels  225 us (52%)
  blocking collectives  88.7 us (21%)
  matrix products  34 us (8%)
  other arithmetic  28.4 us (7%)
  waiting for transfers between devices  21.7 us (5%)
  between operations  14.9 us (3%)
  local copies, waits for them, and re-layouts  11.9 us (3%)
    pallas_call x1, Pallas kernels, backward(): pl.pallas_call(functools.partial(backward_kernel, groups, slots), out_sha...  168 us
    pallas_call x1, Pallas kernels, attend(): pl.pallas_call(functools.partial(attend_kernel, groups, slots), out_shape...  56.6 us
    psum x1, blocking collectives, per_device(): mlp_gain_grad = lax.psum(mlp_gain_half[0], ('seq', 'tp'))  39.1 us
    psum x1, blocking collectives, per_device(): small = lax.psum(small, 'seq')  31.3 us
    psum x1, waiting for transfers between devices, per_device(): lax.psum(tuple((v.astype(BF16) for v in (query_grad, key_grad, value_grad...  21.7 us
    all_gather x1, blocking collectives, per_device(): grad_resid = lax.all_gather(grad_resid_half, 'tp', axis=0, tiled=True)  18.3 us
  transfers between devices with their start and end apart: 2, of which 1 were waited for; matrix products, arithmetic and copies ran while one was open for 6% of the time, Pallas kernels for 0%

profile of v1, /device:TPU:0, one launch (start us, length us, event | category | flops | bytes accessed | tf_op | source)
XLA Modules:
  0.0 424.7 jit_solution(1606399957289280990)
XLA Ops:
  16.7 56.6 %attend.1 = (bf16[4608,128]{1,0:T(8,128)(2,1)}, bf16[1152,896]{1,0:T(8,128)(2,1)}, bf16[1152,896]{1,0:T(8,128)(2,1)}, f32[144,896]{1,0:T(8,128)}, bf16[288,448]{...) custom-call(bf16[288,128]{1,0:T(8,128)(2,1)} %pad_maximum_fusion.1.kv_own, bf16[128,2048]{1,0:T(8,128)(2,1)} %pad.13.qt.qt_in, ...), custom_call_target="tpu_custom_call" | custom-call | tf_op jit(solution)/shard_map/attend/pallas_call | solution.py:1014
  73.3 4.0 fusion.19
  77.4 2.0 fusion.16
  79.4 4.1 multiply_convert_fusion
  83.5 1.9 fusion.18
  85.4 1.9 convolution_convert_fusion.3
  87.4 3.3 convolution_convert_fusion.mlp_part
  90.7 2.9 convolution_convert_fusion.1
  93.5 1.9 convolution_convert_fusion.2
  95.5 3.3 fusion.grad_part
  98.8 1.6 pad_maximum_fusion
  100.4 168.2 %backward.1 = (bf16[288,896]{1,0:T(8,128)(2,1)}, f32[144,896]{1,0:T(8,128)}, f32[64,2048]{1,0:T(8,128)}, f32[288,128]{1,0:T(8,128)}, bf16[4,16,112,640]{3,2,1,0:...) custom-call(bf16[1152,896]{1,0:T(8,128)(2,1)} %fusion.grad_part, ...), custom_call_target="tpu_custom_call" | custom-call | tf_op jit(solution)/shard_map/backward/pallas_call | solution.py:1061
  274.2 1.9 convolution_convert_fusion.6
  278.1 1.6 convolution_convert_fusion.4
  279.8 18.3 %all_gather.3 = f32[288,896]{1,0:T(8,128)S(1)} all-gather(f32[144,896]{1,0:T(8,128)S(1)} %copy-done.9), channel_id=1, replica_groups=mesh['seq'=16,'tp'=2] {'tp'}, dimensions={0}, use_global_device_ids=true | all-gather | bytes 1548288 | tf_op jit(solution)/shard_map/all_gather | solution.py:1269
  298.3 39.1 %psum.55 = f32[896]{0:T(1024)} all-reduce(f32[896]{0:T(1024)S(1)} %reduce.1), channel_id=1, replica_groups=mesh['seq'=16,'tp'=2] {'seq','tp'}, use_global_device_ids=true, to_apply=%region_12.13 | all-reduce | flops 896 | bytes 7168 | tf_op jit(solution)/shard_map/psum | solution.py:1271
  337.4 4.3 %slice_bitcast_fusion.3 = (bf16[896,640]{1,0:T(8,128)(2,1)S(1)}, bf16[896,640]{1,0:T(8,128)(2,1)S(1)}, bf16[896,640]{1,0:T(8,128)(2,1)S(1)}, bf16[896,640]{1,0:T...) fusion(bf16[4,2,896,640]{3,2,1,0:T(8,128)(2,1)} %bitcast.62), kind=kLoop, calls=%fused_computation.36 | loop fusion | bytes 18350080 | tf_op jit(solution)/shard_map/squeeze | solution.py:1236
  342.4 4.1 slice_convert_fusion
  346.5 6.5 %maximum_convert_fusion = (f32[896,2432]{1,0:T(8,128)}, f32[896,2432]{1,0:T(8,128)}) fusion(bf16[896,512]{1,0:T(8,128)(2,1)S(1)} %slice.122, bf16[896,640]{1,0:T(8,128)(2,1)S(1)} %get-tuple-element.59, bf16[896,640]{1,0:T(8,128)(2,1)S(1)} %get-tuple-element.60, bf16[896,640]{1,0:T(8,128)(2,1)S(1)} %get-tuple-element.61, bf16[896,512]{1,0:T(8,128)(2,1)S(1)} %slice.127, ...), kind=kLoop, calls=%fused_computation.4 | loop fusion | flops 34865152 | bytes 26148864 | tf_op jit(solution)/shard_map/convert_element_type | solution.py:1239
  353.0 1.6 fusion.15
  354.7 31.3 %psum.50 = f32[1472]{0:T(1024)S(1)} all-reduce(f32[1472]{0:T(1024)S(1)} %concatenate.47), channel_id=1, replica_groups=mesh['seq'=16,'tp'=2] {'seq'}, use_global_device_ids=true, to_apply=%region_7.8 | all-reduce | flops 1472 | bytes 11776 | tf_op jit(solution)/shard_map/psum | solution.py:1273
  387.8 2.2 fusion.11
  389.9 21.7 %all-reduce.10.cloned.1.call-done = (bf16[896,448]{0,1:T(8,128)(2,1)}, bf16[896,64]{0,1:T(8,128)(2,1)}, bf16[896,64]{0,1:T(8,128)(2,1)}, bf16[448,896]{1,0:T(8,128)(2,1)}) async-done(((bf16[896,448]{0,1:T(8,128)(2,1)}, bf16[896,64]{0,1:T(8,128)(2,1)}, bf16[896,64]{0,1:T(8,128)(2,1)}, bf16[448,896]{1,0:T(8,128)(2,1)}), (bf16[896,448]{0,1:T(8,128)(2,1)}, bf16[896,64]{0,1:T(8,128)(2,1)}, ...) | async-done | bytes 1835024 | tf_op jit(solution)/shard_map/psum | solution.py:1280
  411.6 2.5 convert_element_type.145
  (124 shorter events, 23.1 us)
Async XLA Ops:
  7.2 5.2 %copy-start = (bf16[896,448]{0,1:T(8,128)(2,1)S(1)}, bf16[896,448]{0,1:T(8,128)(2,1)}, u32[]{:S(2)}) copy-start(bf16[896,448]{0,1:T(8,128)(2,1)} %param.18) | copy-start | bytes 2408452
  7.2 5.1 %copy-start.1 = (bf16[288,896]{1,0:T(8,128)(2,1)S(1)}, bf16[288,896]{1,0:T(8,128)(2,1)}, u32[]{:S(2)}) copy-start(bf16[288,896]{1,0:T(8,128)(2,1)} %x_in.1) | copy-start | bytes 1548292
  7.2 4.8 %copy-start.19 = (s32[32]{0:T(128)S(1)}, s32[32]{0:T(128)}, u32[]{:S(2)}) copy-start(s32[32]{0:T(128)} %param.16) | copy-start | bytes 388
  7.2 5.1 %copy-start.16 = (f32[896]{0:T(1024)S(1)}, f32[896]{0:T(1024)}, u32[]{:S(2)}) copy-start(f32[896]{0:T(1024)} %param.17) | copy-start | bytes 10756
  7.2 5.1 %copy-start.21 = (f32[448]{0:T(512)S(1)}, f32[448]{0:T(512)}, u32[]{:S(2)}) copy-start(f32[448]{0:T(512)} %param.19) | copy-start | bytes 5380
  7.2 345.8 %all-reduce.8.cloned.1.call-start = ((), (), s32[]{:S(2)}) async-start(), calls=%async_computation | async-start | bytes 1032192 | tf_op jit(solution)/shard_map/psum | solution.py:1265
  13.3 2.3 copy-start.11
  13.3 2.3 copy-start.22
  16.7 60.6 %slice-start = ((s8[4358144]{0:T(1024)(128)(4,1)}), s8[163840]{0:T(1024)(128)(4,1)S(1)}, s32[]{:S(2)}) async-start(s8[4358144]{0:T(1024)(128)(4,1)} %bitcast.63), calls=%async_computation.2 | async-start | bytes 327680
  73.3 4.0 slice-start.1
  73.3 4.0 copy-start.3
  77.3 6.1 %slice-start.2 = ((s8[4358144]{0:T(1024)(128)(4,1)}), s8[4194304]{0:T(1024)(128)(4,1)S(1)}, s32[]{:S(2)}) async-start(s8[4358144]{0:T(1024)(128)(4,1)} %bitcast.65), calls=%async_computation.4 | async-start | bytes 8388608
  79.3 4.1 slice-start.3
  90.7 4.8 %slice-start.4 = ((s8[4358144]{0:T(1024)(128)(4,1)}), s8[4194304]{0:T(1024)(128)(4,1)S(1)}, s32[]{:S(2)}) async-start(s8[4358144]{0:T(1024)(128)(4,1)} %bitcast.67), calls=%async_computation.6 | async-start | bytes 8388608
  270.4 2.2 copy-start.13
  273.0 3.1 copy-start.4
  274.1 137.5 %all-reduce.10.cloned.1.call-start = ((), (), s32[]{:S(2)}) async-start(), calls=%async_computation.1 | async-start | bytes 3670016 | tf_op jit(solution)/shard_map/psum | solution.py:1280
  279.7 18.6 %copy-start.18 = (f32[1,896]{1,0:T(1,128)S(1)}, f32[1,896]{1,0:T(1,128)}, u32[]{:S(2)}) copy-start(f32[1,896]{1,0:T(1,128)} %get-tuple-element.41) | copy-start | bytes 10756
  337.4 5.0 %slice-start.6 = ((s8[4587520]{0:T(1024)(128)(4,1)}), s8[4194304]{0:T(1024)(128)(4,1)S(1)}, s32[]{:S(2)}) async-start(s8[4587520]{0:T(1024)(128)(4,1)} %bitcast.69), calls=%async_computation.8 | async-start | bytes 8388608
  337.4 5.1 %slice-start.7 = ((s8[4587520]{0:T(1024)(128)(4,1)}), s8[393216]{0:T(1024)(128)(4,1)S(1)}, s32[]{:S(2)}) async-start(s8[4587520]{0:T(1024)(128)(4,1)} %bitcast.69), calls=%async_computation.9 | async-start | bytes 786432
  411.6 2.5 copy-start.15
  411.6 3.2 copy-start.14
  411.6 3.9 copy-start.6
  414.1 2.7 copy-start.10
  (9 other events, 14.0 us)
Sparse Core Ops, SparseCore 0:
  274.3 34.2 all-reduce.7
  314.1 97.5 all-reduce.9

commit v2 on v1

--- a/solution.py
+++ b/solution.py
@@ -13,7 +13,10 @@
 ROPE_BASE = 1000000.0
 LANES = 128
 QUAD = 4
-GRAIN = 8
+WIDE_ROWS = 64
+TALL_ROWS = 64
+SHARE = (4, 3, 3, 4, 1, 1, 2, 3, 2, 2, 4, 1, 2, 1, 2)
+PACE = 4
 MESH = pl.DeviceIdType.MESH
 VMEM_LIMIT = 60 * 1024 * 1024
 BF16 = jnp.bfloat16
@@ -412,6 +415,7 @@
             self.x_send,
             self.c_recv,
             self.c_send,
+            self.keep,
         ) = sems
 
     def root(self, parity):
@@ -420,105 +424,69 @@
     def lag_up(self, parity):
         groups, group, root = self.place.groups, self.place.group, self.root(parity)
         most = max(root, groups - 1 - root)
-        return jnp.where(
+        return PACE * jnp.where(
             group < root, group, jnp.where(group > root, groups - 1 - group, most)
         )
 
     def lag_down(self, parity):
         groups, group, root = self.place.groups, self.place.group, self.root(parity)
         most = max(root, groups - 1 - root)
-        return most + jnp.abs(group - root)
+        return PACE * (most + jnp.abs(group - root))
 
     def total_steps(self):
         groups = self.place.groups
         most = groups // 2
-        return self.count + 2 * most + 2
-
-    def spread(self, i):
-        place = self.place
-        view = self.final.at[place.quad, i]
-        send(view, view, self.x_send.at[i], self.x_recv.at[i], place.across)
-        send(view, view, self.c_send.at[0, i], self.c_recv.at[0, i], place.sibling)
+        return self.count + PACE * (2 * most + 1)
+
+    def spread(self, i, view):
+        place = self.place
+        final = self.final.at[place.quad, i]
+        send(view, final, self.x_send.at[i], self.x_recv.at[i], place.across)
+        send(view, final, self.c_send.at[0, i], self.c_recv.at[0, i], place.sibling)
 
     def up(self, i, parity):
         place, root = self.place, self.root(parity)
         group, last = place.group, place.groups - 1
         mine = self.own.at[i]
 
+        def add(way):
+            neighbour = place.in_group(group - 1 + 2 * way)
+            arrived(self.incoming.at[way, i], self.up_recv.at[way, i], neighbour)
+            mine[...] = (mine[...].astype(F32) + self.incoming[way, i].astype(F32)).astype(BF16)
+
+        def onward(way, dst, send_sem, recv_sem):
+            send(mine, dst, send_sem, recv_sem, place.in_group(group + 1 - 2 * way))
+
         @pl.when((group > 0) & (group <= root))
         def from_left():
-            arrived(self.incoming.at[i], self.up_recv.at[0, i], place.in_group(group - 1))
-            mine[...] = (mine[...].astype(F32) + self.incoming[i].astype(F32)).astype(BF16)
-
-        @pl.when((group < last) & (group > root))
+            add(0)
+
+        @pl.when((group < last) & (group >= root))
         def from_right():
-            arrived(self.incoming.at[i], self.up_recv.at[1, i], place.in_group(group + 1))
-            mine[...] = (mine[...].astype(F32) + self.incoming[i].astype(F32)).astype(BF16)
+            add(1)
 
         @pl.when(group < root)
         def to_right():
-            send(
-                mine,
-                self.incoming.at[i],
-                self.up_send.at[i],
-                self.up_recv.at[0, i],
-                place.in_group(group + 1),
-            )
-
-        @pl.when(group > root + 1)
+            onward(0, self.incoming.at[0, i], self.up_send.at[i], self.up_recv.at[0, i])
+
+        @pl.when(group > root)
         def to_left():
-            send(
-                mine,
-                self.incoming.at[i],
-                self.up_send.at[i],
-                self.up_recv.at[1, i],
-                place.in_group(group - 1),
-            )
-
-        @pl.when(group == root + 1)
-        def to_root():
-            send(
-                mine,
-                self.final.at[place.quad, i],
-                self.up_send.at[i],
-                self.up_recv.at[1, i],
-                place.in_group(group - 1),
-            )
+            onward(1, self.incoming.at[1, i], self.up_send.at[i], self.up_recv.at[1, i])
 
         @pl.when(group == root)
         def at_root():
-            view = self.final.at[place.quad, i]
-
-            @pl.when(group < last)
-            def both():
-                arrived(view, self.up_recv.at[1, i], place.in_group(group + 1))
-                view[...] = (mine[...].astype(F32) + view[...].astype(F32)).astype(BF16)
-
-            @pl.when(group == last)
-            def alone():
-                view[...] = mine[...]
+            final = self.final.at[place.quad, i]
 
             @pl.when(group > 0)
             def left():
-                send(
-                    view,
-                    view,
-                    self.fin_send.at[0, i],
-                    self.fin_recv.at[i],
-                    place.in_group(group - 1),
-                )
+                onward(1, final, self.fin_send.at[0, i], self.fin_recv.at[i])
 
             @pl.when(group < last)
             def right():
-                send(
-                    view,
-                    view,
-                    self.fin_send.at[1, i],
-                    self.fin_recv.at[i],
-                    place.in_group(group + 1),
-                )
-
-            self.spread(i)
+                onward(0, final, self.fin_send.at[1, i], self.fin_recv.at[i])
+
+            self.spread(i, mine)
+            pltpu.make_async_copy(mine, final, self.keep.at[i]).start()
 
     def down(self, i, parity):
         place, root = self.place, self.root(parity)
@@ -549,7 +517,7 @@
                     place.in_group(group + 1),
                 )
 
-            self.spread(i)
+            self.spread(i, view)
 
     def cross(self, i):
         place = self.place
@@ -573,7 +541,7 @@
                 self.down(i, parity)
 
         for parity in (0, 1):
-            i = number - self.lag_down(parity) - 1
+            i = number - self.lag_down(parity) - PACE
 
             @pl.when((i >= 0) & (i < self.count) & (i % 2 == parity))
             def go_cross(i=i):
@@ -594,6 +562,11 @@
             @pl.when(group != root)
             def up_done():
                 sent(view, self.up_send.at[i], place.sibling)
+
+            @pl.when(group == root)
+            def kept():
+                final = self.final.at[place.quad, i]
+                pltpu.make_async_copy(view, final, self.keep.at[i]).wait()
 
             @pl.when((group <= root) & (group > 0))
             def left_done():
@@ -622,6 +595,7 @@
         dma((count,)),
         dma((2, count)),
         dma((2, count)),
+        dma((count,)),
     ]
 
 
@@ -727,6 +701,158 @@
         sent(self.last_in.at[:, self.cut :], self.sems.at[12], place.partner)
 
 
+class QuadSum:
+    def __init__(self, place, part, own, core_in, x_send, x_in, sems):
+        self.place, self.part, self.own = place, part, own
+        self.core_in, self.x_send, self.x_in, self.sems = core_in, x_send, x_in, sems
+
+    def start(self):
+        place = self.place
+        for side in (0, 1):
+            send(
+                self.part.at[side * 2 + 1 - place.core],
+                self.core_in.at[side],
+                self.sems.at[side],
+                self.sems.at[2 + side],
+                place.sibling,
+            )
+
+    def total(self, side):
+        return self.part[side * 2 + self.place.core].astype(F32) + self.core_in[side].astype(F32)
+
+    def middle(self):
+        place = self.place
+        for side in (0, 1):
+            arrived(self.core_in.at[side], self.sems.at[2 + side], place.sibling)
+        self.x_send[...] = self.total(1 - place.side).astype(BF16)
+        send(self.x_send, self.x_in, self.sems.at[4], self.sems.at[5], place.across)
+
+    def end(self):
+        place = self.place
+        arrived(self.x_in, self.sems.at[5], place.across)
+        mine = (self.total(place.side) + self.x_in[...].astype(F32)).astype(BF16)
+        count, step = self.own.shape[0], self.own.shape[1]
+        for i in range(count):
+            piece = mine[i * step : (i + 1) * step, :]
+            if piece.shape[0]:
+                self.own[i, : piece.shape[0], :] = piece
+            if piece.shape[0] < step:
+                left = step - piece.shape[0]
+                self.own[i, piece.shape[0] :, :] = jnp.zeros((left, piece.shape[1]), BF16)
+
+    def finish(self):
+        place = self.place
+        for side in (0, 1):
+            sent(self.core_in.at[side], self.sems.at[side], place.sibling)
+        sent(self.x_send, self.sems.at[4], place.across)
+
+
+class ColumnSum:
+    def __init__(self, place, own, incoming, final, sems):
+        self.place, self.own, self.incoming, self.final = place, own, incoming, final
+        self.rs_send, self.rs_recv, self.ag_send, self.ag_recv = (sems.at[i] for i in range(4))
+        self.x_send, self.x_recv, self.c_send, self.c_recv = (sems.at[i] for i in range(4, 8))
+        self.d_send, self.d_recv = (sems.at[i] for i in range(8, 10))
+
+    def others(self):
+        place = self.place
+        for step in range(1, place.groups):
+            yield step, (place.group + step) % place.groups
+
+    def start(self):
+        place = self.place
+        for step, other in self.others():
+            back = place.groups - step
+            send(
+                self.own.at[other],
+                self.incoming.at[back],
+                self.rs_send.at[step],
+                self.rs_recv.at[back],
+                place.in_group(other),
+            )
+
+    def spread(self, part, view):
+        place = self.place
+        final = self.final.at[place.quad, part]
+        send(view, final, self.x_send.at[part], self.x_recv.at[part], place.across)
+        send(view, final, self.c_send.at[part], self.c_recv.at[part], place.sibling)
+
+    def middle(self):
+        place = self.place
+        mine = self.own.at[place.group]
+        total = mine[...].astype(F32)
+        for step, other in self.others():
+            arrived(self.incoming.at[step], self.rs_recv.at[step], place.sibling)
+            total = total + self.incoming[step].astype(F32)
+        mine[...] = total.astype(BF16)
+        final = self.final.at[place.quad, place.group]
+        for step, other in self.others():
+            send(
+                mine,
+                final,
+                self.ag_send.at[step],
+                self.ag_recv.at[place.group],
+                place.in_group(other),
+            )
+        self.spread(place.group, mine)
+        pltpu.make_async_copy(mine, final, self.ag_send.at[0]).start()
+
+    def end(self):
+        place = self.place
+        for step, other in self.others():
+            view = self.final.at[place.quad, other]
+            arrived(view, self.ag_recv.at[other], place.sibling)
+            self.spread(other, view)
+
+    def cross(self):
+        place = self.place
+        quad = place.across[0] % QUAD
+        for step in range(place.groups):
+            part = (place.group + step) % place.groups
+            view = self.final.at[quad, part]
+            arrived(view, self.x_recv.at[part], place.across)
+            send(view, view, self.d_send.at[part], self.d_recv.at[part], place.sibling)
+
+    def finish(self):
+        place = self.place
+        view = self.own.at[0]
+        for part in range(place.groups):
+            arrived(view, self.c_recv.at[part], place.sibling)
+            arrived(view, self.d_recv.at[part], place.sibling)
+            sent(view, self.x_send.at[part], place.across)
+            sent(view, self.c_send.at[part], place.sibling)
+            sent(view, self.d_send.at[part], place.sibling)
+        for step, other in self.others():
+            sent(view, self.rs_send.at[step], place.sibling)
+            sent(view, self.ag_send.at[step], place.sibling)
+        final = self.final.at[place.quad, place.group]
+        pltpu.make_async_copy(self.own.at[place.group], final, self.ag_send.at[0]).wait()
+
+
+def column_parts(groups, rows, columns):
+    return (groups, round_up(-(-rows // groups), 16), columns)
+
+
+def column_sum_scratch(groups, rows, columns):
+    parts = column_parts(groups, rows, columns)
+    return [
+        *quad_sum_scratch(rows, columns),
+        pltpu.VMEM(parts, BF16),
+        pltpu.VMEM(parts, BF16),
+        pltpu.SemaphoreType.DMA((10, groups)),
+    ]
+
+
+def quad_sum_scratch(rows, columns):
+    return [
+        pltpu.VMEM((QUAD, rows, columns), BF16),
+        pltpu.VMEM((2, rows, columns), BF16),
+        pltpu.VMEM((rows, columns), BF16),
+        pltpu.VMEM((rows, columns), BF16),
+        pltpu.SemaphoreType.DMA((6,)),
+    ]
+
+
 def layer_sum_scratch(half, columns):
     cut = columns // LANES // 2 * LANES
     if cut * 2 < columns:
@@ -758,23 +884,32 @@
     lse,
     qt_in,
     kv_all,
+    x_in,
+    attn_gain,
+    weights_in,
+    cosine,
+    sine,
     layer_out,
-    resid_grad,
-    dq_out,
-    dkv_out,
+    input_grad,
     wide,
     tall,
-    out_grad,
-    gain_grad,
+    outs,
+    ins_q,
+    ins_kv,
+    gains,
+    biases,
     *scratch,
 ):
     place = Place(groups)
     wide_own, tall_own, wide_up, tall_up = scratch[0:4]
-    wide_sems, tall_sems = scratch[4:12], scratch[12:20]
-    sum_g, sum_m = scratch[20:27], scratch[27:34]
-    branch, qt, dot_t, q_pad, do_pad, dkv = scratch[34:40]
-    sib_send, sib_in, x_send, x_in, z_send, z_in = scratch[40:46]
-    kv_sems, pair_sems = scratch[46:48]
+    wide_sems, tall_sems = scratch[4:13], scratch[13:22]
+    sum_g, sum_m = scratch[22:29], scratch[29:36]
+    branch, qt, dot_t, q_pad, do_pad, dkv = scratch[36:42]
+    sib_send, sib_in, side_send, side_in, z_send, z_in = scratch[42:48]
+    kv_sems, pair_sems = scratch[48:50]
+    dq_out, dkv_out, resid_grad = scratch[50:53]
+    turn_send, turn_in, gain_in, bias_in, gain_z, bias_z, vector_sems = scratch[53:60]
+    sum_o, sum_q, sum_kv = scratch[60:68], scratch[68:76], scratch[76:84]
     rows = att.shape[0]
     half = rows // 2
     span = 2 * rows
@@ -795,11 +930,27 @@
     ]
     for fill in fills:
         fill.start()
+
+    def quad_and_column(final, refs):
+        quad = QuadSum(place, refs[0], refs[5], *refs[1:5])
+        return quad, ColumnSum(place, refs[5], refs[6], final, refs[7])
+
+    outs_quad, outs_sum = quad_and_column(outs, sum_o)
+    q_quad, q_sum = quad_and_column(ins_q, sum_q)
+    kv_quad, kv_sum = quad_and_column(ins_kv, sum_kv)
     tall_steps = tall_sum.count
 
     def chain_step(number):
         tall_sum.step(number)
         wide_sum.step(number - tall_steps)
+
+    def chain_steps(first, count):
+        def one(number, unused):
+            chain_step(number)
+            return unused
+
+        lax.fori_loop(first, first + count, one, 0)
+        return first + count
 
     all_steps = tall_steps + wide_sum.total_steps()
 
@@ -807,8 +958,7 @@
     grad_sum.start()
     for fill in fills:
         fill.wait()
-    chain_step(0)
-    mlp_sum.start()
+    done = chain_steps(0, SHARE[0])
 
     qt[...] = qt_in[...]
     at = HEAD_DIM + slots
@@ -818,17 +968,17 @@
 
     grad_sum.after_core()
     grad_sum.cross()
-    chain_step(1)
-    mlp_sum.after_core()
+    mlp_sum.start()
+    done = chain_steps(done, SHARE[1])
     grad_sum.after_cross()
-    mlp_sum.cross()
-    chain_step(2)
+    done = chain_steps(done, SHARE[2])
 
     resid = resid_in[...]
     factor = lax.rsqrt(jnp.mean(resid * resid, axis=-1, keepdims=True) + EPSILON)
     normed = resid * factor
     grad_normed = grad_sum.result()
-    gain_grad[...] = jnp.sum(grad_normed * normed, axis=0, keepdims=True)
+    features = resid.shape[1]
+    gains[:, features:] = jnp.sum(grad_normed * normed, axis=0, keepdims=True)
     weighted = grad_normed * gain[...]
     inner = jnp.mean(weighted * normed, axis=-1, keepdims=True)
     grad_resid = cot[my_rows, :].astype(F32) + factor * (weighted - normed * inner)
@@ -841,13 +991,15 @@
         pair_sems.at[1],
         place.partner,
     )
-    mlp_sum.after_cross()
-    chain_step(3)
-    chain_step(4)
+    mlp_sum.after_core()
+    mlp_sum.cross()
+    done = chain_steps(done, SHARE[3])
     arrived(branch.at[other_rows], pair_sems.at[1], place.partner)
 
     grads = branch[...]
-    out_grad[...] = tn(att[...], grads)
+    outs_part = sum_o[0]
+    outs_part[...] = tn(att[...], grads).astype(BF16).reshape(outs_part.shape)
+    outs_quad.start()
     grad_att = nt(grads, out_weight[...]).astype(BF16)
     stacked = jnp.concatenate(
         [grad_att[:, head * HEAD_DIM : (head + 1) * HEAD_DIM] for head in range(heads)]
@@ -859,15 +1011,19 @@
     delta = jnp.sum(turned * ot[...], axis=0, keepdims=True)
     dot_t[0:HEAD_DIM, :] = split_rows(-delta, 0, HEAD_DIM)
     dot_t[HEAD_DIM:, :] = turned.astype(BF16)
-    chain_step(5)
-    layer_out[my_rows, :] = (resid + mlp_sum.result()).astype(BF16)
-    send(
-        layer_out.at[my_rows],
-        layer_out.at[my_rows],
-        pair_sems.at[2],
-        pair_sems.at[3],
-        place.partner,
-    )
+    done = chain_steps(done, SHARE[4])
+    outs_quad.middle()
+
+    def write_layer():
+        layer_out[my_rows, :] = (resid_in[...] + mlp_sum.result()).astype(BF16)
+        send(
+            layer_out.at[my_rows],
+            layer_out.at[my_rows],
+            pair_sems.at[2],
+            pair_sems.at[3],
+            place.partner,
+        )
+
     dq_out[...] = jnp.zeros_like(dq_out)
 
     def chunk_place(number):
@@ -919,17 +1075,17 @@
         mine = pl.ds(pl.multiple_of(place.core * rows, 16), rows)
         total = dkv[1 if near else 0, mine, :] + sib_in[number].astype(F32)
         if not near:
-            x_send[step] = total.astype(BF16)
+            side_send[step] = total.astype(BF16)
             send(
-                x_send.at[step],
-                x_in.at[step],
+                side_send.at[step],
+                side_in.at[step],
                 kv_sems.at[2, step],
                 kv_sems.at[3, step],
                 place.across,
             )
             return
-        arrived(x_in.at[step], kv_sems.at[3, step], place.across)
-        total = total + x_in[step].astype(F32)
+        arrived(side_in.at[step], kv_sems.at[3, step], place.across)
+        total = total + side_in[step].astype(F32)
         if own_group:
             dkv_out[...] = total
             return
@@ -943,10 +1099,12 @@
             place.in_group(group),
         )
 
+    each = 2
+
     def pair(step, unused):
         attend_back(2 * step, 0)
         hand_over(2 * step, 0)
-        chain_step(6 + 2 * step)
+        chain_steps(done + 2 * each * step, each)
 
         @pl.when(step > 0)
         def last_near():
@@ -955,30 +1113,179 @@
         attend_back(2 * step + 1, 1)
         hand_over(2 * step + 1, 1)
         take_over(2 * step, False)
-        chain_step(7 + 2 * step)
+        chain_steps(done + 2 * each * step + each, each)
+
+        @pl.when(step == 0)
+        def outs_ready():
+            mlp_sum.after_cross()
+            outs_quad.end()
+            outs_sum.start()
+
+        @pl.when(step == 1)
+        def layer_ready():
+            write_layer()
+            outs_sum.middle()
+
         return unused
 
     lax.fori_loop(0, groups - 1, pair, 0)
+    outs_sum.end()
+    done += 2 * each * (groups - 1)
     attend_back(chunks - 2, 0)
     hand_over(chunks - 2, 0)
-    chain_step(6 + 2 * (groups - 1))
+    done = chain_steps(done, each)
     if groups > 1:
         take_over(chunks - 3, True)
     attend_back(chunks - 1, 1, True)
     hand_over(chunks - 1, 1)
     take_over(chunks - 2, False)
-    chain_step(7 + 2 * (groups - 1))
+    done = chain_steps(done, SHARE[5])
+
+    quarter = HEAD_DIM // 2
+    raw = dq_out[...] * HEAD_DIM**-0.5
+    one, two = raw[:quarter, :], raw[quarter:, :]
+    cos, sin = cosine[...], sine[...]
+    turned = jnp.concatenate([one * cos + two * sin, two * cos - one * sin], axis=0)
+    natural = jnp.transpose(turned).astype(BF16)
+    grad_query = jnp.concatenate(
+        [natural[head * rows : (head + 1) * rows, :] for head in range(heads)], axis=1
+    )
+    x_all = x_in[...].astype(F32)
+    factor_all = lax.rsqrt(jnp.mean(x_all * x_all, axis=-1, keepdims=True) + EPSILON)
+    normed_attn = (x_all * factor_all * attn_gain[...]).astype(BF16)
+    wide_q = grad_query.shape[1]
+    q_part = sum_q[0]
+    q_part[...] = tn(normed_attn, grad_query).astype(BF16).reshape(q_part.shape)
+    q_quad.start()
+    turn_send[...] = nt(grad_query, weights_in[:, :wide_q])
+    biases[...] = jnp.zeros_like(biases)
+    biases[:, :wide_q] = jnp.sum(grad_query.astype(F32), axis=0, keepdims=True)
+    done = chain_steps(done, SHARE[11])
     take_over(chunks - 1, True, True)
+    q_quad.middle()
+    outs_sum.cross()
+    done = chain_steps(done, SHARE[6])
     for step in range(groups - 1):
         arrived(z_in.at[step], kv_sems.at[5, step], place.sibling)
         dkv_out[...] += z_in[step].astype(F32)
-
-    def rest(number, unused):
+    turned = jnp.transpose(dkv_out[...])
+    one, two = turned[:quarter, :], turned[quarter:HEAD_DIM, :]
+    cos, sin = cosine[:, :rows], sine[:, :rows]
+    turned = jnp.concatenate(
+        [one * cos + two * sin, two * cos - one * sin, turned[HEAD_DIM:, :]], axis=0
+    )
+    grad_kv = jnp.transpose(turned).astype(BF16)
+    kv_part = sum_kv[0]
+    kv_part[...] = tn(normed_attn, grad_kv).astype(BF16).reshape(kv_part.shape)
+    kv_quad.start()
+    turn_send[...] += nt(grad_kv, weights_in[:, wide_q:])
+    turn_in[0] = turn_send[other_rows, :].astype(BF16)
+    send(turn_in.at[0], turn_in.at[1], vector_sems.at[0], vector_sems.at[1], place.partner)
+    biases[:, wide_q : wide_q + LANES] = jnp.sum(grad_kv.astype(F32), axis=0, keepdims=True)
+    done = chain_steps(done, SHARE[12])
+    kv_quad.middle()
+    q_quad.end()
+    q_sum.start()
+    done = chain_steps(done, SHARE[7])
+    kv_quad.end()
+    kv_sum.start()
+    x_half = x_in[my_rows, :].astype(F32)
+    factor = lax.rsqrt(jnp.mean(x_half * x_half, axis=-1, keepdims=True) + EPSILON)
+    normed = x_half * factor
+    done = chain_steps(done, SHARE[13])
+    arrived(turn_in.at[1], vector_sems.at[1], place.partner)
+    grad_normed = turn_send[my_rows, :] + turn_in[1].astype(F32)
+    gains[:, :features] = jnp.sum(grad_normed * normed, axis=0, keepdims=True)
+    weighted = grad_normed * attn_gain[...]
+    mean = jnp.mean(weighted * normed, axis=-1, keepdims=True)
+    input_grad[my_rows, :] = (
+        resid_grad[...] + factor * (weighted - normed * mean)
+    ).astype(BF16)
+
+    def vectors(hop, device, with_biases):
+        send(gains, gain_in.at[hop], vector_sems.at[4 + 4 * hop], vector_sems.at[5 + 4 * hop], device)
+        if with_biases:
+            send(
+                biases,
+                bias_in.at[hop],
+                vector_sems.at[6 + 4 * hop],
+                vector_sems.at[7 + 4 * hop],
+                device,
+            )
+
+    def vectors_done(hop, device, with_biases):
+        arrived(gain_in.at[hop], vector_sems.at[5 + 4 * hop], device)
+        sent(gains, vector_sems.at[4 + 4 * hop], device)
+        gains[...] += gain_in[hop]
+        if with_biases:
+            arrived(bias_in.at[hop], vector_sems.at[7 + 4 * hop], device)
+            sent(biases, vector_sems.at[6 + 4 * hop], device)
+            biases[...] += bias_in[hop]
+
+    hops = ((place.partner, False), (place.sibling, True), (place.across, True))
+    vectors(0, *hops[0])
+    send(
+        input_grad.at[my_rows],
+        input_grad.at[my_rows],
+        vector_sems.at[2],
+        vector_sems.at[3],
+        place.partner,
+    )
+    done = chain_steps(done, SHARE[14])
+    q_sum.middle()
+    vectors_done(0, *hops[0])
+    vectors(1, *hops[1])
+    kv_sum.middle()
+    done = chain_steps(done, SHARE[8])
+    vectors_done(1, *hops[1])
+    vectors(2, *hops[2])
+    done = chain_steps(done, SHARE[9])
+    vectors_done(2, *hops[2])
+    gain_z[place.group] = gains[...]
+    bias_z[place.group] = biases[...]
+    base = 16
+    for step in range(1, groups):
+        other = place.in_group((place.group + step) % groups)
+        for number, ref in enumerate((gain_z, bias_z)):
+            send(
+                ref.at[place.group],
+                ref.at[place.group],
+                vector_sems.at[base + 4 * step + 2 * number],
+                vector_sems.at[base + 4 * (groups - step) + 2 * number + 1],
+                other,
+            )
+    q_sum.end()
+    kv_sum.end()
+    done = chain_steps(done, SHARE[10])
+    q_sum.cross()
+    kv_sum.cross()
+    for step in range(1, groups):
+        other = (place.group + groups - step) % groups
+        for number, ref in enumerate((gain_z, bias_z)):
+            arrived(
+                ref.at[other],
+                vector_sems.at[base + 4 * (groups - step) + 2 * number + 1],
+                place.sibling,
+            )
+            sent(
+                ref.at[place.group],
+                vector_sems.at[base + 4 * step + 2 * number],
+                place.sibling,
+            )
+    gains[...] = jnp.sum(gain_z[...], axis=0)
+    biases[...] = jnp.sum(bias_z[...], axis=0)
+
+    def last(number, unused):
         chain_step(number)
         return unused
 
-    lax.fori_loop(8 + 2 * (groups - 1), all_steps, rest, 0)
-
+    lax.fori_loop(done, all_steps, last, 0)
+
+    arrived(input_grad.at[other_rows], vector_sems.at[3], place.partner)
+    sent(input_grad.at[my_rows], vector_sems.at[2], place.partner)
+    sent(turn_in.at[0], vector_sems.at[0], place.partner)
+    for part in (outs_quad, q_quad, kv_quad, outs_sum, q_sum, kv_sum):
+        part.finish()
     arrived(layer_out.at[other_rows], pair_sems.at[3], place.partner)
     sent(branch.at[my_rows], pair_sems.at[0], place.partner)
     sent(branch.at[my_rows], pair_sems.at[2], place.partner)
@@ -989,7 +1296,7 @@
     for number in range(chunks):
         sent(sib_send.at[number], kv_sems.at[0, number], place.sibling)
     for step in range(groups):
-        sent(x_send.at[step], kv_sems.at[2, step], place.across)
+        sent(side_send.at[step], kv_sems.at[2, step], place.across)
     for step in range(groups - 1):
         sent(z_send.at[step], kv_sems.at[4, step], place.sibling)
 
@@ -1048,35 +1355,41 @@
     )(kv_own, qt, x_in, out_weight, gain, cot)
 
 
-def backward(groups, slots, grad_part, mlp_part, wide, tall, resid, cot, gain, out_weight, att, ot, lse, qt, kv_all):
+def backward(groups, slots, operands):
+    (grad_part, mlp_part, wide, tall, resid, cot, gain, out_weight, att, ot, lse, qt, kv_all) = (
+        operands[:13]
+    )
+    weights_in = operands[15]
     rows, inner = att.shape
     half = rows // 2
     features = grad_part.shape[1]
-    total = kv_all.shape[0]
     width, queries = qt.shape
     chunks = 2 * groups
+    both = round_up(weights_in.shape[1], LANES)
     dma = pltpu.SemaphoreType.DMA
     shape = jax.ShapeDtypeStruct
     pass_shape = (rows, LANES)
+    outs = (inner // QUAD, features)
+    ins_q = (features // QUAD, inner)
+    ins_kv = (features // QUAD, weights_in.shape[1] - inner)
     return pl.pallas_call(
         functools.partial(backward_kernel, groups, slots),
         out_shape=[
             shape((rows, features), BF16),
-            shape((half, features), F32),
-            shape((HEAD_DIM, queries), F32),
-            shape((rows, LANES), F32),
+            shape((rows, features), BF16),
             shape((QUAD, *wide.shape), BF16),
             shape((QUAD, *tall.shape), BF16),
-            shape((inner, features), F32),
-            shape((1, features), F32),
+            *(shape((QUAD, *column_parts(groups, *dims)), BF16) for dims in (outs, ins_q, ins_kv)),
+            shape((1, 2 * features), F32),
+            shape((1, both), F32),
         ],
-        in_specs=vmem_specs(2) + [pl.BlockSpec(memory_space=pl.ANY)] * 2 + vmem_specs(9),
-        out_specs=vmem_specs(8),
+        in_specs=vmem_specs(2) + [pl.BlockSpec(memory_space=pl.ANY)] * 2 + vmem_specs(14),
+        out_specs=vmem_specs(2) + [pl.BlockSpec(memory_space=pl.ANY)] * 5 + vmem_specs(2),
         scratch_shapes=[
             pltpu.VMEM(wide.shape, BF16),
             pltpu.VMEM(tall.shape, BF16),
-            pltpu.VMEM(wide.shape, BF16),
-            pltpu.VMEM(tall.shape, BF16),
+            pltpu.VMEM((2, *wide.shape), BF16),
+            pltpu.VMEM((2, *tall.shape), BF16),
             *chain_sems(wide.shape[0]),
             *chain_sems(tall.shape[0]),
             *layer_sum_scratch(half, features),
@@ -1095,10 +1408,23 @@
             pltpu.VMEM((groups, *pass_shape), BF16),
             dma((6, chunks)),
             dma((6,)),
+            pltpu.VMEM((HEAD_DIM, queries), F32),
+            pltpu.VMEM((rows, LANES), F32),
+            pltpu.VMEM((half, features), F32),
+            pltpu.VMEM((rows, features), F32),
+            pltpu.VMEM((2, half, features), BF16),
+            pltpu.VMEM((3, 1, 2 * features), F32),
+            pltpu.VMEM((3, 1, both), F32),
+            pltpu.VMEM((groups, 1, 2 * features), F32),
+            pltpu.VMEM((groups, 1, both), F32),
+            dma((16 + 4 * groups + 4,)),
+            *column_sum_scratch(groups, *outs),
+            *column_sum_scratch(groups, *ins_q),
+            *column_sum_scratch(groups, *ins_kv),
         ],
         compiler_params=params(2),
         name="backward",
-    )(grad_part, mlp_part, wide, tall, resid, cot, gain, out_weight, att, ot, lse, qt, kv_all)
+    )(*operands)
 
 
 def rope_tables(positions, head_size):
@@ -1116,13 +1442,6 @@
     return jnp.concatenate(
         [first * cosine - second * sine, second * cosine + first * sine], axis=-1
     )
-
-
-def rms_backward(grad_normed, normed, factor, gain):
-    gain_grad = jnp.sum(grad_normed * normed, axis=0)
-    weighted = grad_normed * gain
-    values_grad = factor * (weighted - normed * jnp.mean(weighted * normed, axis=-1, keepdims=True))
-    return (gain_grad, values_grad)
 
 
 def piece_of(weight, axis, piece, quad):
@@ -1219,13 +1538,24 @@
         + jnp.einsum("rf,df->rd", grad_upward, up_piece, preferred_element_type=F32)
     ).astype(BF16)
     wide = jnp.concatenate([gate_grad.astype(BF16), up_grad.astype(BF16)], axis=0).reshape(
-        2 * GRAIN, features // GRAIN, piece
-    )
-    tall = down_grad.reshape(GRAIN, piece // GRAIN, features)
-
-    layer_output, grad_resid_half, dq, dkv, wide_sum, tall_sum, out_grad, mlp_gain_half = backward(
-        groups, slots, grad_part, mlp_part, wide, tall, resid, out_cotangent, gain_row, out_weight,
-        att, ot, lse, qt, kv_all,
+        2 * features // WIDE_ROWS, WIDE_ROWS, piece
+    )
+    tall = down_grad.reshape(piece // TALL_ROWS, TALL_ROWS, features)
+    weights_in = jnp.concatenate([query_weight, key_weight, value_weight], axis=1)
+    tables = tuple(
+        jnp.pad(
+            jnp.tile(jnp.transpose(table[:, 0, :]), (1, heads)),
+            ((0, 0), (0, queries - heads * rows)),
+        )
+        for table in (cosine, sine)
+    )
+    layer_output, input_grad, wide_sum, tall_sum, outs, ins_q, ins_kv, gains, biases = backward(
+        groups,
+        slots,
+        (
+            grad_part, mlp_part, wide, tall, resid, out_cotangent, gain_row, out_weight,
+            att, ot, lse, qt, kv_all, layer_input, attn_gain[None, :], weights_in, *tables,
+        ),
     )
 
     keep = hidden - (QUAD - 1) * piece
@@ -1241,46 +1571,20 @@
     gate_sum, up_sum = side_by_side(0), side_by_side(1)
     down_sum = tall_sum.reshape(QUAD * piece, features)[:hidden].astype(F32)
 
-    grad_query_rot = jnp.transpose(
-        dq[:, : heads * rows].reshape(HEAD_DIM, heads, rows), (2, 1, 0)
-    ) * scale
-    grad_query = rotate(grad_query_rot, cosine, -sine).reshape(rows, -1).astype(BF16)
-    grad_key = (
-        rotate(dkv[:, :HEAD_DIM].reshape(rows, 1, HEAD_DIM), cosine, -sine)
-        .reshape(rows, HEAD_DIM)
-        .astype(BF16)
-    )
-    grad_value = dkv[:, HEAD_DIM:].astype(BF16)
-    query_grad = jnp.einsum("rd,rh->dh", normed_attn, grad_query, preferred_element_type=F32)
-    key_grad = jnp.einsum("rd,rh->dh", normed_attn, grad_key, preferred_element_type=F32)
-    value_grad = jnp.einsum("rd,rh->dh", normed_attn, grad_value, preferred_element_type=F32)
-    query_bias_grad = jnp.sum(grad_query.astype(F32), axis=0)
-    key_bias_grad = jnp.sum(grad_key.astype(F32), axis=0)
-    value_bias_grad = jnp.sum(grad_value.astype(F32), axis=0)
-    grad_normed_attn = (
-        jnp.einsum("rh,dh->rd", grad_query, query_weight, preferred_element_type=F32)
-        + jnp.einsum("rh,dh->rd", grad_key, key_weight, preferred_element_type=F32)
-        + jnp.einsum("rh,dh->rd", grad_value, value_weight, preferred_element_type=F32)
-    )
-    grad_normed_attn = lax.psum(grad_normed_attn.astype(BF16), "tp").astype(F32)
-    attn_gain_grad, grad_input_part = rms_backward(
-        grad_normed_attn, normed_first, factor_first, attn_gain
-    )
-    grad_resid = lax.all_gather(grad_resid_half, "tp", axis=0, tiled=True)
-    input_grad = (grad_resid + grad_input_part).astype(BF16)
-    mlp_gain_grad = lax.psum(mlp_gain_half[0], ("seq", "tp"))
-    small = jnp.concatenate([attn_gain_grad, query_bias_grad, key_bias_grad, value_bias_grad])
-    small = lax.psum(small, "seq")
-    attn_gain_grad = small[:features]
-    query_bias_grad = small[features : features + heads * HEAD_DIM]
-    key_bias_grad = small[features + heads * HEAD_DIM : features + (heads + 1) * HEAD_DIM]
-    value_bias_grad = small[features + (heads + 1) * HEAD_DIM :]
-    query_grad, key_grad, value_grad, out_grad = (
-        value.astype(F32)
-        for value in lax.psum(
-            tuple(v.astype(BF16) for v in (query_grad, key_grad, value_grad, out_grad)), "seq"
-        )
-    )
+    query_width = heads * HEAD_DIM
+
+    def quarters(parts, row_count):
+        parts = parts.reshape(QUAD, -1, parts.shape[-1])[:, : row_count // QUAD]
+        return parts.reshape(row_count, -1).astype(F32)
+
+    out_grad = quarters(outs, query_width)
+    query_grad = quarters(ins_q, features)
+    key_value = quarters(ins_kv, features)
+    key_grad, value_grad = key_value[:, :HEAD_DIM], key_value[:, HEAD_DIM:]
+    attn_gain_grad, mlp_gain_grad = gains[0, :features], gains[0, features:]
+    query_bias_grad = biases[0, :query_width]
+    key_bias_grad = biases[0, query_width : query_width + HEAD_DIM]
+    value_bias_grad = biases[0, query_width + HEAD_DIM : query_width + 2 * HEAD_DIM]
     return (
         layer_output,
         input_grad,

time: 430 us -> 277 us (0.64)
  blocking collectives: 88.7 us -> 0 us
  waiting for transfers between devices: 21.7 us -> 0 us
  Pallas kernels: 225 us -> 204 us
  between operations: 14.9 us -> 1.36 us
  other arithmetic: 28.4 us -> 19.9 us
  local copies, waits for them, and re-layouts: 11.9 us -> 18.3 us
  matrix products: 34 us -> 28.6 us
    psum x2 -> x0, blocking collectives: 70.4 us -> none  [the longest x1 39.1 us: per_device(): mlp_gain_grad = lax.psum(mlp_gain_half[0], ('seq', 'tp'))]
    psum x2 -> x0, waiting for transfers between devices: 21.7 us -> none  [the longest x1 21.7 us: per_device(): lax.psum(tuple((v.astype(BF16) for v in (query_grad, key_grad, value_grad...]
    pallas_call x1, Pallas kernels: 168 us -> 147 us  [backward(): pl.pallas_call(functools.partial(backward_kernel, groups, slots), out_sha...]
    all_gather x1 -> x0, blocking collectives: 18.3 us -> none  [per_device(): grad_resid = lax.all_gather(grad_resid_half, 'tp', axis=0, tiled=True)]
    convert_element_type x6 -> x3, other arithmetic: 8.29 us -> 1.67 us  [quarters(): return parts.reshape(row_count, -1).astype(F32)]
    dot_general x6 -> x0, matrix products: 6.45 us -> none  [the longest x1 1.91 us: per_device(): jnp.einsum('rd,rh->dh', normed_attn, grad_key, preferred_element_type=F32)]
  transfers between devices with their start and end apart: 2 -> 0, of which waited for: 1 -> 0; matrix products, arithmetic and copies ran while one was open for 6% -> 0% of each run, Pallas kernels for 0% -> 0%
where the time goes in v2:
time: 277 us; the launch traced here: 272 us
  Pallas kernels  204 us (74%)
  matrix products  28.6 us (10%)
  other arithmetic  19.9 us (7%)
  local copies, waits for them, and re-layouts  18.3 us (7%)
    pallas_call x1, Pallas kernels, backward(): pl.pallas_call(functools.partial(backward_kernel, groups, slots), out_sha...  147 us
    pallas_call x1, Pallas kernels, attend(): pl.pallas_call(functools.partial(attend_kernel, groups, slots), out_shape...  56.6 us
    convert_element_type x1, other arithmetic, side_by_side(): return jnp.concatenate(parts, axis=1).astype(F32)  6.97 us

profile of v2, /device:TPU:0, one launch (start us, length us, event | category | flops | bytes accessed | tf_op | source)
XLA Modules:
  0.0 272.0 jit_solution(12182783714811518031)
XLA Ops:
  1.8 1.2 fusion.4
  3.1 1.8 convolution_add_fusion.1
  6.6 0.9 pad.20.qt.qt_in
  10.3 56.6 %attend.1 = (bf16[4608,128]{1,0:T(8,128)(2,1)}, bf16[1152,896]{1,0:T(8,128)(2,1)}, bf16[1152,896]{1,0:T(8,128)(2,1)}, f32[144,896]{1,0:T(8,128)}, bf16[288,448]{...) custom-call(bf16[288,128]{1,0:T(8,128)(2,1)} %pad_maximum_fusion.2.kv_own, bf16[128,2048]{1,0:T(8,128)(2,1)} %pad.20.qt.qt_in, ...), custom_call_target="tpu_custom_call" | custom-call | tf_op jit(solution)/shard_map/attend/pallas_call | solution.py:1321
  66.9 4.0 %fusion.7 = f32[1152,640]{1,0:T(8,128)S(1)} fusion(bf16[1152,896]{1,0:T(8,128)(2,1)} %get-tuple-element.30, s32[]{:T(128)S(6)} %select_n.26, bf16[2432,896]{1,0:T(8,128)(2,1)} %param.28), kind=kOutput, calls=%fused_computation.40 | convolution fusion | flops 1321205760 | bytes 9371652 | tf_op jit(solution)/shard_map/rd,fd->rf/dot_general | solution.py:1529
  70.9 3.7 %fusion.10 = f32[1152,640]{1,0:T(8,128)S(1)} fusion(bf16[1152,896]{1,0:T(8,128)(2,1)} %get-tuple-element.31, s32[]{:T(128)S(6)} %select_n.26, bf16[896,2432]{1,0:T(8,128)(2,1)S(1)} %bitcast.66), kind=kOutput, calls=%fused_computation.43 | convolution fusion | flops 1321205760 | bytes 9371652 | tf_op jit(solution)/shard_map/dot_general | solution.py:1522
  74.6 3.2 %multiply_convert_fusion = (bf16[1152,640]{1,0:T(8,128)(2,1)S(1)}, bf16[1152,640]{1,0:T(8,128)(2,1)S(1)}, bf16[1152,640]{1,0:T(8,128)(2,1)S(1)}) fusion(f32[1152,640]{1,0:T(8,128)S(1)} %fusion.10, f32[1152,640]{1,0:T(8,128)S(1)} %fusion.7, bf16[1152,896]{1,0:T(8,128)(2,1)S(1)} %copy-done.15, s32[]{:T(128)S(6)} %select_n.26, bf16[896,2432]{1,0:T(8,128)(2,1)S(1)} %bitcast.68), kind=kOutput, calls=%fused_computation.9 | convolution fusion | flops 1332264960 | bytes 16744452 | tf_op jit(solution)/shard_map/dot_general | solution.py:1523
  77.8 1.9 convolution_convert_fusion.3
  79.7 1.9 convolution_convert_fusion.2
  81.7 1.6 pad_maximum_fusion
  83.3 0.8 copy-done.1
  84.1 2.9 %convolution_convert_fusion.1 = bf16[640,896]{1,0:T(8,128)(2,1)} fusion(bf16[1152,640]{1,0:T(8,128)(2,1)S(1)} %get-tuple-element.86, bf16[1152,896]{1,0:T(8,128)(2,1)S(1)} %copy-done.1), kind=kOutput, calls=%fused_computation.15 | convolution fusion | flops 1321779200 | bytes 4685824 | tf_op jit(solution)/shard_map/rf,rd->fd/dot_general | solution.py:1528
  87.0 1.9 fusion.9
  88.9 3.3 %fusion.grad_part = bf16[1152,896]{1,0:T(8,128)(2,1)} fusion(f32[1152,896]{1,0:T(8,128)S(1)} %fusion.9, bf16[1152,640]{1,0:T(8,128)(2,1)S(1)} %get-tuple-element.88, s32[]{:T(128)S(6)} %select_n.26, bf16[896,2432]{1,0:T(8,128)(2,1)S(1)} %bitcast.68), kind=kOutput, calls=%fused_computation.7 | convolution fusion | flops 1323270144 | bytes 12025860 | tf_op jit(solution)/shard_map/rf,df->rd/dot_general | solution.py:1538
  92.2 3.3 %convolution_convert_fusion.mlp_part = bf16[1152,896]{1,0:T(8,128)(2,1)} fusion(bf16[1152,640]{1,0:T(8,128)(2,1)S(1)} %get-tuple-element.86, s32[]{:T(128)S(6)} %select_n.26, bf16[2432,896]{1,0:T(8,128)(2,1)S(1)} %bitcast.64), kind=kOutput, calls=%fused_computation.8 | convolution fusion | flops 1322237952 | bytes 7897092 | tf_op jit(solution)/shard_map/dot_general | solution.py:1527
  98.6 1.3 pad_maximum_fusion.1.weights_in
  100.5 147.2 %backward.1 = (bf16[288,896]{1,0:T(8,128)(2,1)}, bf16[288,896]{1,0:T(8,128)(2,1)}, bf16[4,28,64,640]{3,2,1,0:T(8,128)(2,1)}, bf16[4,10,64,896]{3,2,1,0:T(8,128)(...) custom-call(bf16[1152,896]{1,0:T(8,128)(2,1)} %fusion.grad_part, ...), custom_call_target="tpu_custom_call" | custom-call | tf_op jit(solution)/shard_map/backward/pallas_call | solution.py:1375
  247.7 4.1 %slice_bitcast_fusion.3 = (bf16[896,640]{1,0:T(8,128)(2,1)S(1)}, bf16[896,640]{1,0:T(8,128)(2,1)S(1)}, bf16[896,640]{1,0:T(8,128)(2,1)S(1)}, bf16[896,640]{1,0:T...) fusion(bf16[4,2,896,640]{3,2,1,0:T(8,128)(2,1)} %bitcast.61), kind=kLoop, calls=%fused_computation.24 | loop fusion | bytes 18350080 | tf_op jit(solution)/shard_map/squeeze | solution.py:1566
  252.0 7.0 %maximum_convert_fusion = (f32[896,2432]{1,0:T(8,128)}, f32[896,2432]{1,0:T(8,128)}) fusion(bf16[896,512]{1,0:T(8,128)(2,1)S(1)} %slice.113, bf16[896,640]{1,0:T(8,128)(2,1)S(1)} %get-tuple-element.83, bf16[896,640]{1,0:T(8,128)(2,1)S(1)} %get-tuple-element.84, bf16[896,640]{1,0:T(8,128)(2,1)S(1)} %get-tuple-element.85, bf16[896,512]{1,0:T(8,128)(2,1)S(1)} %slice.118, ...), kind=kLoop, calls=%fused_computation.4 | loop fusion | flops 34865152 | bytes 26148864 | tf_op jit(solution)/shard_map/convert_element_type | solution.py:1569
  258.9 4.1 %slice_convert_fusion = f32[2432,896]{1,0:T(8,128)} fusion(bf16[2560,896]{1,0:T(8,128)(2,1)S(1)} %bitcast.71), kind=kLoop, calls=%fused_computation.3 | loop fusion | flops 2179072 | bytes 13074432 | tf_op jit(solution)/shard_map/convert_element_type | solution.py:1572
  263.4 1.6 copy.61
  265.1 1.3 bitcast_convert_fusion.1
  266.7 0.9 copy.57
  267.6 0.9 copy.58
  (103 shorter events, 13.4 us)
Async XLA Ops:
  5.4 2.1 copy-start
  5.4 2.1 copy-start.8
  5.4 2.1 copy-start.12
  5.4 2.1 copy-start.16
  6.2 2.4 copy-start.9
  6.2 2.4 copy-start.17
  6.6 3.0 %copy-start.11 = (f32[896]{0:T(1024)S(1)}, f32[896]{0:T(1024)}, u32[]{:S(2)}) copy-start(f32[896]{0:T(1024)} %param.25) | copy-start | bytes 10756
  10.2 60.6 %slice-start.2 = ((s8[4358144]{0:T(1024)(128)(4,1)}), s8[163840]{0:T(1024)(128)(4,1)S(1)}, s32[]{:S(2)}) async-start(s8[4358144]{0:T(1024)(128)(4,1)} %bitcast.65), calls=%async_computation.2 | async-start | bytes 327680
  66.9 4.0 %slice-start.3 = ((s8[4358144]{0:T(1024)(128)(4,1)}), s8[4194304]{0:T(1024)(128)(4,1)S(1)}, s32[]{:S(2)}) async-start(s8[4358144]{0:T(1024)(128)(4,1)} %bitcast.65), calls=%async_computation.3 | async-start | bytes 8388608
  66.9 7.7 %slice-start.4 = ((s8[4358144]{0:T(1024)(128)(4,1)}), s8[4194304]{0:T(1024)(128)(4,1)S(1)}, s32[]{:S(2)}) async-start(s8[4358144]{0:T(1024)(128)(4,1)} %bitcast.67), calls=%async_computation.4 | async-start | bytes 8388608
  70.9 3.7 %slice-start.5 = ((s8[4358144]{0:T(1024)(128)(4,1)}), s8[163840]{0:T(1024)(128)(4,1)S(1)}, s32[]{:S(2)}) async-start(s8[4358144]{0:T(1024)(128)(4,1)} %bitcast.67), calls=%async_computation.5 | async-start | bytes 327680
  70.9 3.7 %copy-start.15 = (bf16[1152,896]{1,0:T(8,128)(2,1)S(1)}, bf16[1152,896]{1,0:T(8,128)(2,1)}, u32[]{:S(2)}) copy-start(bf16[1152,896]{1,0:T(8,128)(2,1)} %get-tuple-element.31) | copy-start | bytes 6193156
  81.7 2.4 copy-start.1
  87.0 5.2 %slice-start = ((s8[4358144]{0:T(1024)(128)(4,1)}), s8[4194304]{0:T(1024)(128)(4,1)S(1)}, s32[]{:S(2)}) async-start(s8[4358144]{0:T(1024)(128)(4,1)} %bitcast.63), calls=%async_computation | async-start | bytes 8388608
  88.9 3.3 %slice-start.1 = ((s8[4358144]{0:T(1024)(128)(4,1)}), s8[163840]{0:T(1024)(128)(4,1)S(1)}, s32[]{:S(2)}) async-start(s8[4358144]{0:T(1024)(128)(4,1)} %bitcast.63), calls=%async_computation.1 | async-start | bytes 327680
  95.5 2.1 copy-start.3
  251.9 7.0 %slice-start.6 = ((s8[4587520]{0:T(1024)(128)(4,1)}), s8[4194304]{0:T(1024)(128)(4,1)S(1)}, s32[]{:S(2)}) async-start(s8[4587520]{0:T(1024)(128)(4,1)} %bitcast.69), calls=%async_computation.6 | async-start | bytes 8388608
  252.0 7.0 %slice-start.7 = ((s8[4587520]{0:T(1024)(128)(4,1)}), s8[393216]{0:T(1024)(128)(4,1)S(1)}, s32[]{:S(2)}) async-start(s8[4587520]{0:T(1024)(128)(4,1)} %bitcast.69), calls=%async_computation.7 | async-start | bytes 786432
  258.9 4.1 %copy-start.2 = (bf16[4,4,64,448]{3,2,1,0:T(8,128)(2,1)S(1)}, bf16[4,4,64,448]{3,2,1,0:T(8,128)(2,1)}, u32[]{:S(2)}) copy-start(bf16[4,4,64,448]{3,2,1,0:T(8,128)(2,1)} %get-tuple-element.40) | copy-start | bytes 2752516
  263.4 1.6 copy-start.4
  266.4 2.0 copy-start.10
  266.4 2.6 copy-start.13
  266.4 3.8 %copy-start.6 = (bf16[288,896]{1,0:T(8,128)(2,1)S(1)}, bf16[288,896]{1,0:T(8,128)(2,1)}, u32[]{:S(2)}) copy-start(bf16[288,896]{1,0:T(8,128)(2,1)} %get-tuple-element.117) | copy-start | bytes 1548292
  266.5 4.5 %copy-start.5 = (bf16[288,896]{1,0:T(8,128)(2,1)S(1)}, bf16[288,896]{1,0:T(8,128)(2,1)}, u32[]{:S(2)}) copy-start(bf16[288,896]{1,0:T(8,128)(2,1)} %get-tuple-element.118) | copy-start | bytes 1548292
  (2 other events, 2.6 us)
